TPU v7x, 512 devices: a whole 4x8x8 slice. The times are simulated.
512 devices in a mesh: tm: 8 (over z), rows: 64 (over y, x, core).
Axes of the slice: x: 4, y: 8, z: 8, core: 2. Of those that a mesh axis runs over, the one named last changes fastest.
Arguments:
- w_inv: bfloat16 [8, 1536, 1536], P('tm', 'rows'), may hold values from -1 to 1, as said below
- lower_block: bfloat16 [8, 1536, 1536], P('tm', 'rows'), may hold values from -0.15625 to 0.15625
- sigma_end: float32 [1536, 1536], P('rows'), may hold values from -3 to 3, as said below
- chain_break: int32 [8], replicated, may hold values 0 or 1
Outputs:
- sigma_diag: float32 [8, 1536, 1536], P('tm', 'rows')
- sigma_cross: float32 [8, 1536, 1536], P('tm', 'rows')
Inputs may be any that keep to these rules, and one draw needn't show every extreme that they name: w_inv is lower triangular with a positive diagonal. sigma_end is symmetric with a positive diagonal.
All inputs are finite; a program needn't handle non-finite values.
Results may differ from a plain program's by a relative error of at most 0.0045.
Values may be sent and summed in bfloat16 or wider, within the bound.
A program may use at most 64 MiB of HBM per device.

v0:
```python
import jax
import jax.numpy as jnp
from jax import lax
from jax.sharding import PartitionSpec as P


def shifted(value, axis, steps):
    count = lax.axis_size(axis)
    initial, last = (max(0, -steps), min(count, count - steps))
    return lax.ppermute(value, axis, [(source, source + steps) for source in range(initial, last)])


def shards(w_inv, lower_block, sigma_end, chain_break):
    weight_rows = w_inv[0]
    lower_rows = lower_block[0]
    row_count = weight_rows.shape[0]
    width = weight_rows.shape[1]
    my_start = lax.axis_index("rows") * row_count
    contract_first = (((0,), (0,)), ((), ()))
    weight_full = lax.all_gather(weight_rows, "rows", axis=0, tiled=True)
    coupled_rows = jnp.dot(lower_rows, weight_full, preferred_element_type=jnp.float32)
    own_columns = lax.dynamic_slice_in_dim(weight_full, my_start, row_count, 1)
    gram_rows = lax.dot_general(
        own_columns, weight_full, contract_first, preferred_element_type=jnp.float32
    )
    coupled_full = lax.all_gather(coupled_rows.astype(jnp.bfloat16), "rows", axis=0, tiled=True)
    n_parts = lax.axis_size("tm")
    part_index = lax.axis_index("tm")
    flagged = jnp.sum(jnp.where(jnp.arange(n_parts) == part_index, chain_break, 0))
    use_end = jnp.logical_or(flagged == 1, part_index == n_parts - 1)
    end_b = sigma_end.astype(jnp.bfloat16)
    carried = end_b
    sigma_rows = gram_rows
    product = jnp.zeros((row_count, width), jnp.float32)
    for step in range(n_parts):
        source = jnp.where(use_end, end_b, carried)
        product = jnp.dot(source, coupled_full, preferred_element_type=jnp.float32)
        columns = lax.all_to_all(
            product.astype(jnp.bfloat16), "rows", split_axis=1, concat_axis=0, tiled=True
        )
        sigma_rows = gram_rows + lax.dot_general(
            columns, coupled_full, contract_first, preferred_element_type=jnp.float32
        )
        if step + 1 < n_parts:
            carried = shifted(sigma_rows.astype(jnp.bfloat16), "tm", -1)
    return (sigma_rows[None], (-product)[None])


def solution(mesh):
    in_specs = (P("tm", "rows", None), P("tm", "rows", None), P("rows", None), P())
    out_specs = (P("tm", "rows", None), P("tm", "rows", None))
    return jax.shard_map(shards, mesh=mesh, in_specs=in_specs, out_specs=out_specs, check_vma=False)
```

profile of v0, /device:TPU:1, one launch (start us, length us, event | category | flops | bytes accessed | tf_op | source)
XLA Modules:
  0.0 425.8 jit_solution(9045338880063467845)
XLA Ops:
  8.0 93.9 %all-gather.6.cloned.1.call-done = bf16[1,1536,1536]{2,1,0:T(8,128)(2,1)} async-done(((bf16[1,24,1536]{2,1,0:T(8,128)(2,1)}), bf16[1,1536,1536]{2,1,0:T(8,128)(2,1)}) %all-gather.6.cloned.1.call-update) | async-done | bytes 4718608 | tf_op jit(solution)/shard_map/all_gather | solution.py:20
  101.9 3.7 fusion.12
  105.6 82.3 %all-gather.4.cloned.1.call-done = bf16[1536,1536]{1,0:T(8,128)(2,1)} async-done(((bf16[24,1536]{1,0:T(8,128)(2,1)}), bf16[1536,1536]{1,0:T(8,128)(2,1)}) %all-gather.4.cloned.1.call-update) | async-done | bytes 4718608 | tf_op jit(solution)/shard_map/all_gather | solution.py:26
  193.1 6.2 %all-to-all-start = ((bf16[64,2,288]{2,1,0:T(2,128)(2,1)}), bf16[64,2,288]{2,1,0:T(2,128)(2,1)S(1)}, u32[]{:S(2)}, u32[]{:S(2)}) async-start(bf16[64,2,288]{2,1,0:T(2,128)(2,1)} %reshape.30), calls=%async_computation | async-start | bytes 196608 | tf_op jit(solution)/shard_map/all_to_all | solution.py:38
  199.3 3.4 fusion
  202.7 7.1 %all-to-all-done = bf16[64,2,288]{2,1,0:T(2,128)(2,1)S(1)} async-done(((bf16[64,2,288]{2,1,0:T(2,128)(2,1)}), bf16[64,2,288]{2,1,0:T(2,128)(2,1)S(1)}, u32[]{:S(2)}, u32[]{:S(2)}) %all-to-all-start) | async-done | bytes 73760 | tf_op jit(solution)/shard_map/all_to_all | solution.py:38
  210.3 3.1 fusion.5
  218.4 3.0 convolution_convert_fusion.5
  222.9 15.6 %all_to_all.152 = bf16[64,2,288]{2,1,0:T(2,128)(2,1)S(1)} all-to-all(bf16[64,2,288]{2,1,0:T(2,128)(2,1)S(1)} %reshape.32), channel_id=1, replica_groups=mesh['tm'=8,'rows'=64] {'rows'}, dimensions={0} | all-to-all | bytes 147456 | tf_op jit(solution)/shard_map/all_to_all | solution.py:38
  238.9 3.1 fusion.6
  243.2 3.8 collective-permute-done.1
  247.0 3.0 convolution_convert_fusion.4
  251.5 15.5 %all_to_all.153 = bf16[64,2,288]{2,1,0:T(2,128)(2,1)S(1)} all-to-all(bf16[64,2,288]{2,1,0:T(2,128)(2,1)S(1)} %reshape.34), channel_id=1, replica_groups=mesh['tm'=8,'rows'=64] {'rows'}, dimensions={0} | all-to-all | bytes 147456 | tf_op jit(solution)/shard_map/all_to_all | solution.py:38
  267.4 3.1 fusion.7
  271.8 3.8 collective-permute-done.2
  280.1 15.5 %all_to_all.154 = bf16[64,2,288]{2,1,0:T(2,128)(2,1)S(1)} all-to-all(bf16[64,2,288]{2,1,0:T(2,128)(2,1)S(1)} %reshape.36), channel_id=1, replica_groups=mesh['tm'=8,'rows'=64] {'rows'}, dimensions={0} | all-to-all | bytes 147456 | tf_op jit(solution)/shard_map/all_to_all | solution.py:38
  296.0 3.1 fusion.8
  300.4 5.2 %collective-permute-done.3 = bf16[24,1536]{1,0:T(8,128)(2,1)S(1)} collective-permute-done((bf16[24,1536]{1,0:T(8,128)(2,1)S(1)}, bf16[24,1536]{1,0:T(8,128)(2,1)S(1)}, u32[]{:S(2)}, u32[]{:S(2)}) %collective-permute-start.3) | collective-permute-done | bytes 73760 | tf_op jit(solution)/shard_map/ppermute | solution.py:10
  305.5 3.0 convolution_convert_fusion.2
  310.0 14.9 %all_to_all.155 = bf16[64,2,288]{2,1,0:T(2,128)(2,1)S(1)} all-to-all(bf16[64,2,288]{2,1,0:T(2,128)(2,1)S(1)} %reshape.38), channel_id=1, replica_groups=mesh['tm'=8,'rows'=64] {'rows'}, dimensions={0} | all-to-all | bytes 147456 | tf_op jit(solution)/shard_map/all_to_all | solution.py:38
  325.3 3.1 fusion.9
  329.7 5.6 %collective-permute-done.4 = bf16[24,1536]{1,0:T(8,128)(2,1)S(1)} collective-permute-done((bf16[24,1536]{1,0:T(8,128)(2,1)S(1)}, bf16[24,1536]{1,0:T(8,128)(2,1)S(1)}, u32[]{:S(2)}, u32[]{:S(2)}) %collective-permute-start.4) | collective-permute-done | bytes 73760 | tf_op jit(solution)/shard_map/ppermute | solution.py:10
  335.3 3.0 convolution_convert_fusion.1
  339.8 14.9 %all_to_all.156 = bf16[64,2,288]{2,1,0:T(2,128)(2,1)S(1)} all-to-all(bf16[64,2,288]{2,1,0:T(2,128)(2,1)S(1)} %reshape.40), channel_id=1, replica_groups=mesh['tm'=8,'rows'=64] {'rows'}, dimensions={0} | all-to-all | bytes 147456 | tf_op jit(solution)/shard_map/all_to_all | solution.py:38
  355.1 3.1 fusion.10
  359.4 5.6 %collective-permute-done.5 = bf16[24,1536]{1,0:T(8,128)(2,1)S(1)} collective-permute-done((bf16[24,1536]{1,0:T(8,128)(2,1)S(1)}, bf16[24,1536]{1,0:T(8,128)(2,1)S(1)}, u32[]{:S(2)}, u32[]{:S(2)}) %collective-permute-start.5) | collective-permute-done | bytes 73760 | tf_op jit(solution)/shard_map/ppermute | solution.py:10
  369.6 14.9 %all_to_all.157 = bf16[64,2,288]{2,1,0:T(2,128)(2,1)S(1)} all-to-all(bf16[64,2,288]{2,1,0:T(2,128)(2,1)S(1)} %reshape.42), channel_id=1, replica_groups=mesh['tm'=8,'rows'=64] {'rows'}, dimensions={0} | all-to-all | bytes 147456 | tf_op jit(solution)/shard_map/all_to_all | solution.py:38
  384.8 3.1 fusion.11
  389.2 5.6 %collective-permute-done.6 = bf16[24,1536]{1,0:T(8,128)(2,1)S(1)} collective-permute-done((bf16[24,1536]{1,0:T(8,128)(2,1)S(1)}, bf16[24,1536]{1,0:T(8,128)(2,1)S(1)}, u32[]{:S(2)}, u32[]{:S(2)}) %collective-permute-start.6) | collective-permute-done | bytes 73760 | tf_op jit(solution)/shard_map/ppermute | solution.py:10
  394.8 3.7 negate_bitcast_fusion
  400.0 14.9 %all_to_all.158 = bf16[64,2,288]{2,1,0:T(2,128)(2,1)S(1)} all-to-all(bf16[64,2,288]{2,1,0:T(2,128)(2,1)S(1)} %reshape.44), channel_id=1, replica_groups=mesh['tm'=8,'rows'=64] {'rows'}, dimensions={0} | all-to-all | bytes 147456 | tf_op jit(solution)/shard_map/all_to_all | solution.py:38
  415.3 3.8 fusion.4
  (55 shorter events, 37.2 us)
Async XLA Ops:
  7.2 94.7 %copy-start = (bf16[1,24,1536]{2,1,0:T(8,128)(2,1)S(1)}, bf16[1,24,1536]{2,1,0:T(8,128)(2,1)}, u32[]{:S(2)}) copy-start(bf16[1,24,1536]{2,1,0:T(8,128)(2,1)} %param.5) | copy-start | bytes 221188
  7.2 98.4 %copy-start.1 = (f32[24,1536]{1,0:T(8,128)S(1)}, f32[24,1536]{1,0:T(8,128)}, u32[]{:S(2)}) copy-start(f32[24,1536]{1,0:T(8,128)} %param.6) | copy-start | bytes 442372
  7.2 94.7 %all-gather.6.cloned.1.call-start = ((), (), s32[]{:S(2)}) async-start(), calls=%async_computation.9 | async-start | bytes 4792320 | tf_op jit(solution)/shard_map/all_gather | solution.py:20
  7.9 180.0 %all-gather.4.cloned.1.call-start = ((), (), s32[]{:S(2)}) async-start(), calls=%async_computation.8 | async-start | bytes 4792320 | tf_op jit(solution)/shard_map/all_gather | solution.py:26
  193.1 16.8 %all-to-all-start = ((bf16[64,2,288]{2,1,0:T(2,128)(2,1)}), bf16[64,2,288]{2,1,0:T(2,128)(2,1)S(1)}, u32[]{:S(2)}, u32[]{:S(2)}) async-start(bf16[64,2,288]{2,1,0:T(2,128)(2,1)} %reshape.30), calls=%async_computation | async-start | bytes 196608 | tf_op jit(solution)/shard_map/all_to_all | solution.py:38
  199.3 15.3 %copy-start.2 = (s32[8]{0:T(128)S(1)}, s32[8]{0:T(128)}, u32[]{:S(2)}) copy-start(s32[8]{0:T(128)} %param.7) | copy-start | bytes 100
  213.3 5.1 %collective-permute-start = (bf16[24,1536]{1,0:T(8,128)(2,1)S(1)}, bf16[24,1536]{1,0:T(8,128)(2,1)S(1)}, u32[]{:S(2)}, u32[]{:S(2)}) collective-permute-start(bf16[24,1536]{1,0:T(8,128)(2,1)S(1)} %fusion.5), channel_id=1, source_target_pairs={{64,0},{128,64},{192,128},{256,192},{320,256},{384,320},{448,384},... | collective-permute-start | bytes 221192 | tf_op jit(solution)/shard_map/ppermute | solution.py:10
  241.9 5.1 %collective-permute-start.1 = (bf16[24,1536]{1,0:T(8,128)(2,1)S(1)}, bf16[24,1536]{1,0:T(8,128)(2,1)S(1)}, u32[]{:S(2)}, u32[]{:S(2)}) collective-permute-start(bf16[24,1536]{1,0:T(8,128)(2,1)S(1)} %fusion.6), channel_id=1, source_target_pairs={{64,0},{128,64},{192,128},{256,192},{320,256},{384,320},{448,384},... | collective-permute-start | bytes 221192 | tf_op jit(solution)/shard_map/ppermute | solution.py:10
  270.5 5.1 %collective-permute-start.2 = (bf16[24,1536]{1,0:T(8,128)(2,1)S(1)}, bf16[24,1536]{1,0:T(8,128)(2,1)S(1)}, u32[]{:S(2)}, u32[]{:S(2)}) collective-permute-start(bf16[24,1536]{1,0:T(8,128)(2,1)S(1)} %fusion.7), channel_id=1, source_target_pairs={{64,0},{128,64},{192,128},{256,192},{320,256},{384,320},{448,384},... | collective-permute-start | bytes 221192 | tf_op jit(solution)/shard_map/ppermute | solution.py:10
  299.1 6.5 %collective-permute-start.3 = (bf16[24,1536]{1,0:T(8,128)(2,1)S(1)}, bf16[24,1536]{1,0:T(8,128)(2,1)S(1)}, u32[]{:S(2)}, u32[]{:S(2)}) collective-permute-start(bf16[24,1536]{1,0:T(8,128)(2,1)S(1)} %fusion.8), channel_id=1, source_target_pairs={{64,0},{128,64},{192,128},{256,192},{320,256},{384,320},{448,384},... | collective-permute-start | bytes 221192 | tf_op jit(solution)/shard_map/ppermute | solution.py:10
  328.4 6.9 %collective-permute-start.4 = (bf16[24,1536]{1,0:T(8,128)(2,1)S(1)}, bf16[24,1536]{1,0:T(8,128)(2,1)S(1)}, u32[]{:S(2)}, u32[]{:S(2)}) collective-permute-start(bf16[24,1536]{1,0:T(8,128)(2,1)S(1)} %fusion.9), channel_id=1, source_target_pairs={{64,0},{128,64},{192,128},{256,192},{320,256},{384,320},{448,384},... | collective-permute-start | bytes 221192 | tf_op jit(solution)/shard_map/ppermute | solution.py:10
  358.1 6.9 %collective-permute-start.5 = (bf16[24,1536]{1,0:T(8,128)(2,1)S(1)}, bf16[24,1536]{1,0:T(8,128)(2,1)S(1)}, u32[]{:S(2)}, u32[]{:S(2)}) collective-permute-start(bf16[24,1536]{1,0:T(8,128)(2,1)S(1)} %fusion.10), channel_id=1, source_target_pairs={{64,0},{128,64},{192,128},{256,192},{320,256},{384,320},{448,384},... | collective-permute-start | bytes 221192 | tf_op jit(solution)/shard_map/ppermute | solution.py:10
  387.9 6.9 %collective-permute-start.6 = (bf16[24,1536]{1,0:T(8,128)(2,1)S(1)}, bf16[24,1536]{1,0:T(8,128)(2,1)S(1)}, u32[]{:S(2)}, u32[]{:S(2)}) collective-permute-start(bf16[24,1536]{1,0:T(8,128)(2,1)S(1)} %fusion.11), channel_id=1, source_target_pairs={{64,0},{128,64},{192,128},{256,192},{320,256},{384,320},{448,384},... | collective-permute-start | bytes 221192 | tf_op jit(solution)/shard_map/ppermute | solution.py:10
Sparse Core Ops, SparseCore 0:
  11.3 90.4 all-gather.5
  105.8 82.1 all-gather.3
where the time goes:
time: 428 us; the launch traced here: 426 us
  waiting for transfers between devices  216 us (50%)
  blocking collectives  106 us (25%)
  matrix products  57.5 us (13%)
  starting transfers between devices  15.3 us (4%)
  local copies, waits for them, and re-layouts  15.1 us (4%)
  between operations  15 us (4%)
    all_to_all x7, blocking collectives, shards(): lax.all_to_all(product.astype(jnp.bfloat16), 'rows', split_axis=1, concat...  106 us
    all_gather x1, waiting for transfers between devices, shards(): weight_full = lax.all_gather(weight_rows, 'rows', axis=0, tiled=True)  93.9 us
    all_gather x1, waiting for transfers between devices, shards(): lax.all_gather(coupled_rows.astype(jnp.bfloat16), 'rows', axis=0, tiled=T...  82.3 us
    ppermute x7, waiting for transfers between devices, shifted(): lax.ppermute(value, axis, [(source, source + steps) for source in range(i...  32.2 us
    dot_general x8, matrix products, shards(): lax.dot_general(columns, coupled_full, contract_first, preferred_element_...  25.3 us
    dot_general x8, matrix products, shards(): product = jnp.dot(source, coupled_full, preferred_element_type=jnp.float32)  25.1 us
    ppermute x7, starting transfers between devices, shifted(): lax.ppermute(value, axis, [(source, source + steps) for source in range(i...  9.03 us
  transfers between devices with their start and end apart: 10, of which 10 were waited for; matrix products, arithmetic and copies ran while one was open for 1% of the time, Pallas kernels for 0%

commit v1 on v0

v1 whole, which is shorter than its diff:
```python
import jax
import jax.numpy as jnp
from jax import lax
from jax.experimental import pallas as pl
from jax.experimental.pallas import tpu as pltpu
from jax.sharding import PartitionSpec as P

MESH = pl.DeviceIdType.MESH
BF16 = jnp.bfloat16
F32 = jnp.float32
B = 1536
CHIPS = 32
HALF_CHIPS = 16
PANEL = 48
OWN = 24
HALF = 768


def dot(a, b):
    return jnp.dot(a, b, preferred_element_type=F32)


def message(product, j):
    start = PANEL * j
    tile, off = start // 128, start % 128
    lanes = lax.broadcasted_iota(jnp.int32, (PANEL, 128), 1)
    block = product[:, tile * 128:(tile + 1) * 128]
    if off:
        block = pltpu.roll(block, 128 - off, 1)
        if off + PANEL > 128:
            after = pltpu.roll(product[:, (tile + 1) * 128:(tile + 2) * 128], 128 - off, 1)
            block = jnp.where(lanes < 128 - off, block, after)
    top = jnp.where(lanes[:16] < 64, block[:16], pltpu.roll(block[16:32], 64, 1))
    return jnp.concatenate([top, block[32:48]], axis=0).astype(BF16)


def chain(
    flag_ref, coupled_ref, gram_ref, end_ref, sigma_ref, cross_ref,
    end_buf, next_buf, next_out, part_out, part_in, part2_out, part2_in, pack, recv, rows_out,
    end_sem, next_sem, part_sem, part2_sem, rows_sem, pack_send, pack_recv,
):
    parts = 8
    p = lax.axis_index("tm")
    r = lax.axis_index("rows")
    chip, core = r // 2, r % 2
    half = chip // HALF_CHIPS
    place = chip % HALF_CHIPS
    sibling = (p, chip * 2 + 1 - core)

    def peer(j):
        return (p, (core * HALF_CHIPS + j) * 2 + half)

    barrier = pltpu.get_barrier_semaphore()
    pl.semaphore_signal(barrier, 1, device_id=sibling, device_id_type=MESH)

    @pl.when(p > 0)
    def _():
        pl.semaphore_signal(barrier, 1, device_id=(p - 1, r), device_id_type=MESH)

    @pl.when(p < parts - 1)
    def _():
        pl.semaphore_signal(barrier, 1, device_id=(p + 1, r), device_id_type=MESH)

    def is_self(j):
        return jnp.logical_and(core == half, place == j)

    for j in range(HALF_CHIPS):
        @pl.when(jnp.logical_not(is_self(j)))
        def _():
            pl.semaphore_signal(barrier, 1, device_id=peer(j), device_id_type=MESH)

    expected = (
        1 + jnp.where(p > 0, 1, 0) + jnp.where(p < parts - 1, 1, 0)
        + HALF_CHIPS - jnp.where(core == half, 1, 0)
    )
    pl.semaphore_wait(barrier, expected)

    mine = pl.ds(pl.multiple_of(core * HALF, 128), HALF)
    theirs = pl.ds(pl.multiple_of((1 - core) * HALF, 128), HALF)
    my_rows = pl.ds(pl.multiple_of(core * OWN, 8), OWN)
    their_rows = pl.ds(pl.multiple_of((1 - core) * OWN, 8), OWN)

    def to_sibling(src, dst, sems):
        return pltpu.make_async_remote_copy(
            src_ref=src, dst_ref=dst, send_sem=sems.at[0], recv_sem=sems.at[1],
            device_id=sibling, device_id_type=MESH)

    end_copy = to_sibling(end_ref.at[:, theirs], end_buf.at[my_rows], end_sem)
    end_copy.start()
    end_buf[my_rows] = end_ref[:, mine]
    end_copy.wait()

    next_copy = pltpu.make_async_remote_copy(
        src_ref=next_out, dst_ref=next_buf, send_sem=next_sem.at[0], recv_sem=next_sem.at[1],
        device_id=(jnp.maximum(p - 1, 0), r), device_id_type=MESH)

    @pl.when(p < parts - 1)
    def _():
        next_copy.wait_recv()

    @pl.when(p == parts - 1)
    def _():
        next_buf[...] = jnp.zeros_like(next_buf)

    use_end = jnp.logical_or(flag_ref[0] == 1, p == parts - 1)
    source = jnp.where(use_end, end_buf[...].astype(BF16), next_buf[...])

    part_copy = to_sibling(part_out, part_in, part_sem)
    part_out[...] = dot(source, coupled_ref[:, :, theirs].reshape(HALF, HALF))
    part_copy.start()
    product = dot(source, coupled_ref[:, :, mine].reshape(HALF, HALF))
    part_copy.wait_recv()
    product = product + part_in[...]

    def pack_copy(j):
        return pltpu.make_async_remote_copy(
            src_ref=pack.at[j], dst_ref=recv.at[place], send_sem=pack_send.at[j],
            recv_sem=pack_recv.at[place], device_id=peer(j), device_id_type=MESH)

    def arrival(j):
        return pltpu.make_async_remote_copy(
            src_ref=pack.at[j], dst_ref=recv.at[j], send_sem=pack_send.at[j],
            recv_sem=pack_recv.at[j], device_id=peer(j), device_id_type=MESH)

    for j in range(HALF_CHIPS):
        pack[j] = message(product, j)

        @pl.when(jnp.logical_not(is_self(j)))
        def _():
            pack_copy(j).start()

        @pl.when(is_self(j))
        def _():
            recv[j] = pack[j]

    rows_out[0] = -product
    cross_copy = to_sibling(rows_out.at[0, their_rows], cross_ref.at[:, mine], rows_sem.at[0])
    cross_copy.start()
    cross_ref[:, mine] = rows_out[0, my_rows]

    for j in range(HALF_CHIPS):
        @pl.when(jnp.logical_not(is_self(j)))
        def _():
            arrival(j).wait_recv()

    first = recv[:, :16].reshape(HALF_CHIPS * 16, 128).T
    second = recv[:, 16:].reshape(HALF_CHIPS * 16, 128).T

    def update(columns):
        def rows(k):
            return coupled_ref[:, 16 * k:16 * k + 16, columns].reshape(HALF_CHIPS * 16, HALF)
        return dot(first[:48], rows(0)) + dot(first[64:112], rows(1)) + dot(second[:48], rows(2))

    part2_copy = to_sibling(part2_out, part2_in, part2_sem)
    part2_out[...] = update(theirs)
    part2_copy.start()
    sigma = update(mine) + gram_ref[...]
    part2_copy.wait_recv()
    sigma = sigma + part2_in[...]

    @pl.when(p > 0)
    def _():
        next_out[...] = sigma.astype(BF16)
        next_copy.start()

    rows_out[1] = sigma
    sigma_copy = to_sibling(rows_out.at[1, their_rows], sigma_ref.at[:, mine], rows_sem.at[1])
    sigma_copy.start()
    sigma_ref[:, mine] = rows_out[1, my_rows]

    @pl.when(p > 0)
    def _():
        next_copy.wait_send()

    part_copy.wait_send()
    part2_copy.wait_send()
    for j in range(HALF_CHIPS):
        @pl.when(jnp.logical_not(is_self(j)))
        def _():
            pack_copy(j).wait_send()
    cross_copy.wait()
    sigma_copy.wait()


def run_chain(flag, coupled, gram, end):
    vmem = pl.BlockSpec(memory_space=pltpu.VMEM)
    dma = pltpu.SemaphoreType.DMA
    return pl.pallas_call(
        chain,
        out_shape=[jax.ShapeDtypeStruct((OWN, B), F32)] * 2,
        in_specs=[pl.BlockSpec(memory_space=pltpu.SMEM), vmem, vmem, vmem],
        out_specs=[vmem, vmem],
        scratch_shapes=[
            pltpu.VMEM((PANEL, HALF), F32),
            pltpu.VMEM((PANEL, HALF), BF16),
            pltpu.VMEM((PANEL, HALF), BF16),
            pltpu.VMEM((PANEL, HALF), F32),
            pltpu.VMEM((PANEL, HALF), F32),
            pltpu.VMEM((PANEL, HALF), F32),
            pltpu.VMEM((PANEL, HALF), F32),
            pltpu.VMEM((HALF_CHIPS, 32, 128), BF16),
            pltpu.VMEM((HALF_CHIPS, 32, 128), BF16),
            pltpu.VMEM((2, PANEL, HALF), F32),
            dma((2,)), dma((2,)), dma((2,)), dma((2,)), dma((2, 2)),
            dma((HALF_CHIPS,)), dma((HALF_CHIPS,)),
        ],
        compiler_params=pltpu.CompilerParams(
            collective_id=0, has_side_effects=True, vmem_limit_bytes=40 * 1024 * 1024),
    )(flag, coupled, gram, end)


def shards(w_inv, lower_block, sigma_end, chain_break):
    weight_rows = w_inv[0]
    lower_rows = lower_block[0]
    r = lax.axis_index("rows")
    chip, core = r // 2, r % 2
    weight_full = lax.all_gather(weight_rows, "rows", axis=0, tiled=True)
    coupled_rows = jnp.dot(lower_rows, weight_full, preferred_element_type=F32)
    coupled_full = lax.all_gather(coupled_rows.astype(BF16), "rows", axis=0, tiled=True)
    coupled = lax.dynamic_slice_in_dim(coupled_full, core * HALF, HALF, 0)
    own = lax.dynamic_slice_in_dim(weight_full, chip * PANEL, PANEL, 1)
    cols = lax.dynamic_slice_in_dim(weight_full, core * HALF, HALF, 1)
    gram = lax.dot_general(own, cols, (((0,), (0,)), ((), ())), preferred_element_type=F32)
    part = lax.axis_index("tm")
    flag = lax.dynamic_slice_in_dim(chain_break, part, 1, 0)
    sigma, cross = run_chain(flag, coupled.reshape(HALF_CHIPS, PANEL, B), gram, sigma_end)
    return (sigma[None], cross[None])


def solution(mesh):
    in_specs = (P("tm", "rows", None), P("tm", "rows", None), P("rows", None), P())
    out_specs = (P("tm", "rows", None), P("tm", "rows", None))
    return jax.shard_map(shards, mesh=mesh, in_specs=in_specs, out_specs=out_specs, check_vma=False)
```

time: 428 us -> 317 us (0.74)
  Pallas kernels: 0 us -> 117 us
  blocking collectives: 106 us -> 0 us
  matrix products: 57.5 us -> 6.27 us
  waiting for transfers between devices: 216 us -> 174 us
  starting transfers between devices: 15.3 us -> 0.08 us
  local copies, waits for them, and re-layouts: 15.1 us -> 3.75 us
    pallas_call x0 -> x1, Pallas kernels: none -> 117 us  [run_chain(): pl.pallas_call(chain, out_shape=[jax.ShapeDtypeStruct((OWN, B), F32)] * 2...]
    all_to_all x7 -> x0, blocking collectives: 106 us -> none  [shards(): lax.all_to_all(product.astype(jnp.bfloat16), 'rows', split_axis=1, concat...]
    dot_general x18 -> x2, matrix products: 57.5 us -> 6.27 us  [the longest x1 3.71 us: shards(): coupled_rows = jnp.dot(lower_rows, weight_full, preferred_element_type=F32)]
    ppermute x7 -> x0, waiting for transfers between devices: 32.2 us -> none  [shifted(): lax.ppermute(value, axis, [(source, source + steps) for source in range(i...]
    ppermute x7 -> x0, starting transfers between devices: 9.03 us -> none  [shifted(): lax.ppermute(value, axis, [(source, source + steps) for source in range(i...]
    all_to_all x16 -> x0, local copies, waits for them, and re-layouts: 7.12 us -> none  [shards(): lax.all_to_all(product.astype(jnp.bfloat16), 'rows', split_axis=1, concat...]
    all_to_all x1 -> x0, waiting for transfers between devices: 7.12 us -> none  [shards(): lax.all_to_all(product.astype(jnp.bfloat16), 'rows', split_axis=1, concat...]
    unnamed x22 -> x8, local copies, waits for them, and re-layouts: 7.98 us -> 1.34 us
  transfers between devices with their start and end apart: 10 -> 2, of which waited for: 10 -> 2; matrix products, arithmetic and copies ran while one was open for 1% -> 1% of each run, Pallas kernels for 0% -> 0%
where the time goes in v1:
time: 317 us; the launch traced here: 315 us
  waiting for transfers between devices  174 us (55%)
  Pallas kernels  117 us (37%)
  between operations  14.1 us (4%)
  matrix products  6.27 us (2%)
  local copies, waits for them, and re-layouts  3.75 us (1%)
    pallas_call x1, Pallas kernels, run_chain(): pl.pallas_call(chain, out_shape=[jax.ShapeDtypeStruct((OWN, B), F32)] * 2...  117 us
    all_gather x1, waiting for transfers between devices, shards(): weight_full = lax.all_gather(weight_rows, 'rows', axis=0, tiled=True)  93.9 us
    all_gather x1, waiting for transfers between devices, shards(): lax.all_gather(coupled_rows.astype(BF16), 'rows', axis=0, tiled=True)  79.2 us
  transfers between devices with their start and end apart: 2, of which 2 were waited for; matrix products, arithmetic and copies ran while one was open for 1% of the time, Pallas kernels for 0%

profile of v1, /device:TPU:1, one launch (start us, length us, event | category | flops | bytes accessed | tf_op | source)
XLA Modules:
  0.0 315.5 jit_solution(7319341548330094416)
XLA Ops:
  7.2 0.0 copy-start
  7.2 0.0 copy-start.2
  7.2 0.0 all-gather.6.cloned.1.call-start
  7.2 0.7 all-gather.6.cloned.1.call-update
  7.9 0.0 all-gather.4.cloned.1.call-start
  8.0 93.9 %all-gather.6.cloned.1.call-done = bf16[1,1536,1536]{2,1,0:T(8,128)(2,1)} async-done(((bf16[1,24,1536]{2,1,0:T(8,128)(2,1)}), bf16[1,1536,1536]{2,1,0:T(8,128)(2,1)}) %all-gather.6.cloned.1.call-update) | async-done | bytes 4718608 | tf_op jit(solution)/shard_map/all_gather | solution.py:217
  101.9 0.0 copy-done
  101.9 3.7 %fusion.5 = bf16[24,1536]{1,0:T(8,128)(2,1)} fusion(bf16[1,1536,1536]{2,1,0:T(8,128)(2,1)} %all-gather.6.cloned.1.call-done, bf16[1,24,1536]{2,1,0:T(8,128)(2,1)S(1)} %copy-done), kind=kOutput, calls=%fused_computation.5 | convolution fusion | flops 113283072 | bytes 4866048 | tf_op jit(solution)/shard_map/dot_general | solution.py:218
  105.6 0.0 copy-start.1
  105.6 0.0 all-gather.4.cloned.1.call-update
  105.6 0.0 copy-done.2
  105.6 0.6 dynamic_slice.12.flag_ref
  106.2 2.6 fusion.2.gram_ref
  108.8 79.2 %all-gather.4.cloned.1.call-done = bf16[1536,1536]{1,0:T(8,128)(2,1)} async-done(((bf16[24,1536]{1,0:T(8,128)(2,1)}), bf16[1536,1536]{1,0:T(8,128)(2,1)}) %all-gather.4.cloned.1.call-update) | async-done | bytes 4718608 | tf_op jit(solution)/shard_map/all_gather | solution.py:219
  188.0 1.8 constant_dynamic-slice_fusion
  189.8 0.0 copy-done.1
  189.8 117.5 %shard_map.59 = (f32[24,1536]{1,0:T(8,128)S(1)}, f32[24,1536]{1,0:T(8,128)S(1)}) custom-call(s32[1]{0:T(128)} %dynamic_slice.12.flag_ref, bf16[16,48,1536]{2,1,0:T(8,128)(2,1)S(1)} %bitcast.17, f32[48,768]{1,0:T(8,128)S(1)} %fusion.2.gram_ref, f32[24,1536]{1,0:T(8,128)S(1)} %copy-done.1), custom_call_target="tpu_custom_call" | custom-call | tf_op jit(solution)/shard_map/pallas_call | solution.py:188
  307.3 0.7 copy.8
  308.0 0.7 copy.9
Async XLA Ops:
  7.2 94.7 %copy-start = (bf16[1,24,1536]{2,1,0:T(8,128)(2,1)S(1)}, bf16[1,24,1536]{2,1,0:T(8,128)(2,1)}, u32[]{:S(2)}) copy-start(bf16[1,24,1536]{2,1,0:T(8,128)(2,1)} %param.5) | copy-start | bytes 221188
  7.2 98.5 %copy-start.2 = (s32[8]{0:T(128)S(1)}, s32[8]{0:T(128)}, u32[]{:S(2)}) copy-start(s32[8]{0:T(128)} %param.7) | copy-start | bytes 100
  7.2 94.7 %all-gather.6.cloned.1.call-start = ((), (), s32[]{:S(2)}) async-start(), calls=%async_computation.1 | async-start | bytes 4792320 | tf_op jit(solution)/shard_map/all_gather | solution.py:217
  7.9 180.0 %all-gather.4.cloned.1.call-start = ((), (), s32[]{:S(2)}) async-start(), calls=%async_computation | async-start | bytes 4792320 | tf_op jit(solution)/shard_map/all_gather | solution.py:219
  105.6 84.2 %copy-start.1 = (f32[24,1536]{1,0:T(8,128)S(1)}, f32[24,1536]{1,0:T(8,128)}, u32[]{:S(2)}) copy-start(f32[24,1536]{1,0:T(8,128)} %end_ref.1) | copy-start | bytes 442372
Sparse Core Ops, SparseCore 0:
  11.3 90.4 all-gather.5
  105.8 82.1 all-gather.3

commit v2 on v1

--- a/solution.py
+++ b/solution.py
@@ -14,6 +14,7 @@
 PANEL = 48
 OWN = 24
 HALF = 768
+WINDOW = 256
 
 
 def dot(a, b):
@@ -34,9 +35,101 @@
     return jnp.concatenate([top, block[32:48]], axis=0).astype(BF16)
 
 
+class Ring:
+    def __init__(self, buf, sems, p, y, x, core, place, source):
+        self.buf, self.sems = buf, sems
+        self.p, self.y, self.x, self.core = p, y, x, core
+        self.place, self.source = place, source
+        self.sign = 1 - 2 * core
+
+    def copy(self, slot, second, send, receive, y, x):
+        block = self.buf.at[slot, :, HALF * second:HALF * (second + 1)]
+        return pltpu.make_async_remote_copy(
+            src_ref=block, dst_ref=block, send_sem=send, recv_sem=receive,
+            device_id=(self.p, (y * 4 + x) * 2 + self.core), device_id_type=MESH)
+
+    def along_x(self, slot, second, way):
+        sends = self.sems[0].at[slot, second, 1 + way]
+        return self.copy(
+            slot, second, sends, self.sems[1].at[slot, second], self.y, (self.x + way) % 4)
+
+    def along_y(self, slot, second, back):
+        step = -self.sign if back else self.sign
+        sends = self.sems[0].at[slot, second, back]
+        return self.copy(
+            slot, second, sends, self.sems[1].at[slot, second], (self.y + step + 8) % 8, self.x)
+
+    def arrived(self, slot, second):
+        self.along_x(slot, second, 1).wait_recv()
+
+    def columns(self):
+        return [(self.x + i) % 4 for i in (0, 1, 3, 2)]
+
+    def own_sends(self, act):
+        act(self.along_y(self.place, 1, 0))
+        act(self.along_y(self.place, 1, 1))
+        for way in (1, 3, 2):
+            act(self.along_x(self.place, 0, way))
+        act(self.along_y(self.place, 0, 0))
+        act(self.along_y(self.place, 0, 1))
+        for way in (1, 3, 2):
+            act(self.along_x(self.place, 1, way))
+
+    def row_sends(self, act, wait):
+        for column in self.columns()[1:]:
+            slot = (self.y % 4) * 4 + column
+            if wait:
+                self.arrived(slot, 0)
+            act(self.along_y(slot, 0, 0))
+            act(self.along_y(slot, 0, 1))
+
+    def hop(self, act, wait, distance, back):
+        step = self.sign * distance * (1 if back else -1)
+        origin = (self.y + step + 8) % 8
+        last = distance == (3 if back else 4)
+
+        @pl.when(origin // 4 == self.core)
+        def _():
+            row = (origin % 4) * 4
+            slot = row + self.x
+            if wait:
+                self.arrived(slot, 1)
+            if not last:
+                act(self.along_y(slot, 1, back))
+            for way in (1, 3, 2):
+                act(self.along_x(slot, 1, way))
+            for column in self.columns():
+                if wait:
+                    self.arrived(row + column, 0)
+                if not last:
+                    act(self.along_y(row + column, 0, back))
+
+    def walk(self, act, wait):
+        @pl.when(self.source)
+        def _():
+            self.own_sends(act)
+            self.row_sends(act, wait)
+
+        for distance in range(1, 5):
+            self.hop(act, wait, distance, 0)
+            if distance < 4:
+                self.hop(act, wait, distance, 1)
+
+    def run(self):
+        self.walk(lambda copy: copy.start(), True)
+        for s in range(4):
+            for way in (1, 3, 2):
+                self.arrived(s * 4 + (self.x + way) % 4, 1)
+
+    def finish(self):
+        self.walk(lambda copy: copy.wait_send(), False)
+
+
 def chain(
-    flag_ref, coupled_ref, gram_ref, end_ref, sigma_ref, cross_ref,
-    end_buf, next_buf, next_out, part_out, part_in, part2_out, part2_in, pack, recv, rows_out,
+    flag_ref, weight_rows, lower_rows, end_ref, sigma_ref, cross_ref,
+    weight_ref, coupled_ref, weight_out, weight_in, lower_out, lower_buf,
+    coupled_out, coupled_in, gram_buf, end_buf, next_buf, next_out, part_out, part_in, part2_out, part2_in, pack, recv, rows_out,
+    weight_sem, lower_sem, coupled_sem, weight_send, weight_recv, coupled_send, coupled_recv,
     end_sem, next_sem, part_sem, part2_sem, rows_sem, pack_send, pack_recv,
 ):
     parts = 8
@@ -45,6 +138,8 @@
     chip, core = r // 2, r % 2
     half = chip // HALF_CHIPS
     place = chip % HALF_CHIPS
+    y, x = chip // 4, chip % 4
+    source_core = core == half
     sibling = (p, chip * 2 + 1 - core)
 
     def peer(j):
@@ -69,8 +164,17 @@
         def _():
             pl.semaphore_signal(barrier, 1, device_id=peer(j), device_id_type=MESH)
 
+    for around in (1, 7):
+        there = ((y + around) % 8) * 4 + x
+        pl.semaphore_signal(
+            barrier, 1, device_id=(p, there * 2 + core), device_id_type=MESH)
+    for around in (1, 2, 3):
+        there = y * 4 + (x + around) % 4
+        pl.semaphore_signal(
+            barrier, 1, device_id=(p, there * 2 + core), device_id_type=MESH)
+
     expected = (
-        1 + jnp.where(p > 0, 1, 0) + jnp.where(p < parts - 1, 1, 0)
+        6 + jnp.where(p > 0, 1, 0) + jnp.where(p < parts - 1, 1, 0)
         + HALF_CHIPS - jnp.where(core == half, 1, 0)
     )
     pl.semaphore_wait(barrier, expected)
@@ -88,7 +192,54 @@
     end_copy = to_sibling(end_ref.at[:, theirs], end_buf.at[my_rows], end_sem)
     end_copy.start()
     end_buf[my_rows] = end_ref[:, mine]
-    end_copy.wait()
+
+    weight_out[...] = weight_rows[...].astype(F32)
+    weight_copy = to_sibling(weight_out, weight_in.at[my_rows], weight_sem)
+
+    @pl.when(jnp.logical_not(source_core))
+    def _():
+        weight_copy.start()
+
+    lower_out[...] = lower_rows[...].astype(F32)
+    lower_copy = to_sibling(lower_out.at[:, theirs], lower_buf.at[my_rows], lower_sem)
+    lower_copy.start()
+    lower_buf[my_rows] = lower_out[:, mine]
+
+    weight_ring = Ring(weight_ref, (weight_send, weight_recv), p, y, x, core, place, source_core)
+    coupled_ring = Ring(
+        coupled_ref, (coupled_send, coupled_recv), p, y, x, core, place, source_core)
+
+    @pl.when(source_core)
+    def _():
+        weight_in[my_rows] = weight_out[...]
+        weight_copy.wait_recv()
+        weight_ref[place] = weight_in[...].astype(BF16)
+
+    weight_ring.run()
+    lower_copy.wait_recv()
+    lower = lower_buf[...].astype(BF16)
+
+    def coupled_copy(k):
+        columns = pl.ds(HALF * k, HALF)
+        return to_sibling(
+            coupled_out.at[:, columns], coupled_in.at[:, columns], coupled_sem.at[k])
+
+    for k in range(2):
+        coupled_out[:, HALF * k:HALF * (k + 1)] = dot(
+            lower, weight_ref[:, :, HALF * k:HALF * (k + 1)].reshape(HALF, HALF))
+
+        @pl.when(jnp.logical_not(source_core))
+        def _():
+            coupled_copy(k).start()
+
+    @pl.when(source_core)
+    def _():
+        for k in range(2):
+            coupled_copy(k).wait_recv()
+        coupled_ref[place] = (coupled_out[...] + coupled_in[...]).astype(BF16)
+
+    coupled_ring.run()
+    end_copy.wait_recv()
 
     next_copy = pltpu.make_async_remote_copy(
         src_ref=next_out, dst_ref=next_buf, send_sem=next_sem.at[0], recv_sem=next_sem.at[1],
@@ -102,7 +253,7 @@
     def _():
         next_buf[...] = jnp.zeros_like(next_buf)
 
-    use_end = jnp.logical_or(flag_ref[0] == 1, p == parts - 1)
+    use_end = jnp.logical_or(flag_ref[p] == 1, p == parts - 1)
     source = jnp.where(use_end, end_buf[...].astype(BF16), next_buf[...])
 
     part_copy = to_sibling(part_out, part_in, part_sem)
@@ -138,6 +289,13 @@
     cross_copy.start()
     cross_ref[:, mine] = rows_out[0, my_rows]
 
+    window = jnp.minimum(chip * PANEL // 128, (B - WINDOW) // 128) * 128
+    own = weight_ref[:, :, pl.ds(pl.multiple_of(window, 128), WINDOW)].reshape(HALF, WINDOW).T
+    for k in range(B // WINDOW):
+        gram_buf[:, WINDOW * k:WINDOW * (k + 1)] = dot(
+            own, weight_ref[:, :, WINDOW * k:WINDOW * (k + 1)].reshape(HALF, WINDOW))
+    gram_rows = pl.ds(pl.multiple_of(chip * PANEL - window, 16), PANEL)
+
     for j in range(HALF_CHIPS):
         @pl.when(jnp.logical_not(is_self(j)))
         def _():
@@ -149,12 +307,14 @@
     def update(columns):
         def rows(k):
             return coupled_ref[:, 16 * k:16 * k + 16, columns].reshape(HALF_CHIPS * 16, HALF)
-        return dot(first[:48], rows(0)) + dot(first[64:112], rows(1)) + dot(second[:48], rows(2))
+        return (
+            gram_buf[gram_rows, columns]
+            + dot(first[:48], rows(0)) + dot(first[64:112], rows(1)) + dot(second[:48], rows(2)))
 
     part2_copy = to_sibling(part2_out, part2_in, part2_sem)
     part2_out[...] = update(theirs)
     part2_copy.start()
-    sigma = update(mine) + gram_ref[...]
+    sigma = update(mine)
     part2_copy.wait_recv()
     sigma = sigma + part2_in[...]
 
@@ -172,6 +332,17 @@
     def _():
         next_copy.wait_send()
 
+    end_copy.wait_send()
+    lower_copy.wait_send()
+
+    @pl.when(jnp.logical_not(source_core))
+    def _():
+        weight_copy.wait_send()
+        for k in range(2):
+            coupled_copy(k).wait_send()
+
+    weight_ring.finish()
+    coupled_ring.finish()
     part_copy.wait_send()
     part2_copy.wait_send()
     for j in range(HALF_CHIPS):
@@ -182,7 +353,7 @@
     sigma_copy.wait()
 
 
-def run_chain(flag, coupled, gram, end):
+def run_chain(flag, weight, lower, end):
     vmem = pl.BlockSpec(memory_space=pltpu.VMEM)
     dma = pltpu.SemaphoreType.DMA
     return pl.pallas_call(
@@ -191,6 +362,15 @@
         in_specs=[pl.BlockSpec(memory_space=pltpu.SMEM), vmem, vmem, vmem],
         out_specs=[vmem, vmem],
         scratch_shapes=[
+            pltpu.VMEM((HALF_CHIPS, PANEL, B), BF16),
+            pltpu.VMEM((HALF_CHIPS, PANEL, B), BF16),
+            pltpu.VMEM((OWN, B), F32),
+            pltpu.VMEM((PANEL, B), F32),
+            pltpu.VMEM((OWN, B), F32),
+            pltpu.VMEM((PANEL, HALF), F32),
+            pltpu.VMEM((PANEL, B), F32),
+            pltpu.VMEM((PANEL, B), F32),
+            pltpu.VMEM((WINDOW, B), F32),
             pltpu.VMEM((PANEL, HALF), F32),
             pltpu.VMEM((PANEL, HALF), BF16),
             pltpu.VMEM((PANEL, HALF), BF16),
@@ -201,29 +381,19 @@
             pltpu.VMEM((HALF_CHIPS, 32, 128), BF16),
             pltpu.VMEM((HALF_CHIPS, 32, 128), BF16),
             pltpu.VMEM((2, PANEL, HALF), F32),
+            dma((2,)), dma((2,)), dma((2, 2)),
+            dma((HALF_CHIPS, 2, 5)), dma((HALF_CHIPS, 2)),
+            dma((HALF_CHIPS, 2, 5)), dma((HALF_CHIPS, 2)),
             dma((2,)), dma((2,)), dma((2,)), dma((2,)), dma((2, 2)),
             dma((HALF_CHIPS,)), dma((HALF_CHIPS,)),
         ],
         compiler_params=pltpu.CompilerParams(
             collective_id=0, has_side_effects=True, vmem_limit_bytes=40 * 1024 * 1024),
-    )(flag, coupled, gram, end)
+    )(flag, weight, lower, end)
 
 
 def shards(w_inv, lower_block, sigma_end, chain_break):
-    weight_rows = w_inv[0]
-    lower_rows = lower_block[0]
-    r = lax.axis_index("rows")
-    chip, core = r // 2, r % 2
-    weight_full = lax.all_gather(weight_rows, "rows", axis=0, tiled=True)
-    coupled_rows = jnp.dot(lower_rows, weight_full, preferred_element_type=F32)
-    coupled_full = lax.all_gather(coupled_rows.astype(BF16), "rows", axis=0, tiled=True)
-    coupled = lax.dynamic_slice_in_dim(coupled_full, core * HALF, HALF, 0)
-    own = lax.dynamic_slice_in_dim(weight_full, chip * PANEL, PANEL, 1)
-    cols = lax.dynamic_slice_in_dim(weight_full, core * HALF, HALF, 1)
-    gram = lax.dot_general(own, cols, (((0,), (0,)), ((), ())), preferred_element_type=F32)
-    part = lax.axis_index("tm")
-    flag = lax.dynamic_slice_in_dim(chain_break, part, 1, 0)
-    sigma, cross = run_chain(flag, coupled.reshape(HALF_CHIPS, PANEL, B), gram, sigma_end)
+    sigma, cross = run_chain(chain_break, w_inv[0], lower_block[0], sigma_end)
     return (sigma[None], cross[None])
 
 

time: 317 us -> 194 us (0.61)
  waiting for transfers between devices: 174 us -> 0 us
  Pallas kernels: 117 us -> 188 us
  between operations: 14.1 us -> 0.65 us
  matrix products: 6.27 us -> 0 us
    all_gather x2 -> x0, waiting for transfers between devices: 173 us -> none  [the longest x1 93.9 us: shards(): weight_full = lax.all_gather(weight_rows, 'rows', axis=0, tiled=True)]
    pallas_call x1, Pallas kernels: 117 us -> 188 us  [run_chain(): pl.pallas_call(chain, out_shape=[jax.ShapeDtypeStruct((OWN, B), F32)] * 2...]
    dot_general x2 -> x0, matrix products: 6.27 us -> none  [the longest x1 3.71 us: shards(): coupled_rows = jnp.dot(lower_rows, weight_full, preferred_element_type=F32)]
    unnamed x8 -> x10, local copies, waits for them, and re-layouts: 1.34 us -> 4.65 us
  transfers between devices with their start and end apart: 2 -> 0, of which waited for: 2 -> 0; matrix products, arithmetic and copies ran while one was open for 1% -> 0% of each run, Pallas kernels for 0% -> 0%
where the time goes in v2:
time: 194 us
  Pallas kernels  188 us (97%)
  local copies, waits for them, and re-layouts  4.65 us (2%)
    pallas_call x1, Pallas kernels, run_chain(): pl.pallas_call(chain, out_shape=[jax.ShapeDtypeStruct((OWN, B), F32)] * 2...  188 us
    unnamed x10, local copies, waits for them, and re-layouts  4.65 us

profile of v2, /device:TPU:1, one launch (start us, length us, event | category | flops | bytes accessed | tf_op | source)
XLA Modules:
  0.0 193.8 jit_solution(9346500747331281298)
XLA Ops:
  0.6 0.0 copy-start.3
  0.6 0.6 copy-done.3
  1.3 0.0 copy-start
  1.3 0.9 copy-done
  2.2 0.0 copy-start.1
  2.2 0.9 copy-done.1
  3.1 0.0 copy-start.2
  3.1 0.9 copy-done.2
  4.0 188.5 %shard_map.59 = (f32[24,1536]{1,0:T(8,128)S(1)}, f32[24,1536]{1,0:T(8,128)S(1)}) custom-call(s32[8]{0:T(128)S(1)} %copy-done.3, bf16[24,1536]{1,0:T(8,128)(2,1)S(1)} %bitcast.6, bf16[24,1536]{1,0:T(8,128)(2,1)S(1)} %bitcast.7, f32[24,1536]{1,0:T(8,128)S(1)} %copy-done), custom_call_target="tpu_custom_call" | custom-call | tf_op jit(solution)/shard_map/pallas_call | solution.py:359
  192.4 0.7 copy.8
  193.1 0.7 copy.9
Async XLA Ops:
  0.6 0.7 copy-start.3
  1.3 0.9 copy-start
  2.2 0.9 copy-start.1
  3.1 0.9 copy-start.2

commit v3 on v1

--- a/solution.py
+++ b/solution.py
@@ -14,6 +14,7 @@
 PANEL = 48
 OWN = 24
 HALF = 768
+WINDOW = 256
 
 
 def dot(a, b):
@@ -34,9 +35,164 @@
     return jnp.concatenate([top, block[32:48]], axis=0).astype(BF16)
 
 
+class Ring:
+    def __init__(self, lower, weight, sems, p, y, x, core, place, source):
+        self.lower, self.weight = lower, weight
+        self.sends, self.receives, self.over, self.came = sems
+        self.p, self.y, self.x, self.core = p, y, x, core
+        self.place, self.source = place, source
+        self.sign = 1 - 2 * core
+
+    def block(self, slot, kind, core):
+        if kind == 0:
+            return self.lower.at[slot]
+        return self.weight.at[HALF_CHIPS * core + slot, :, HALF * (kind - 1):HALF * kind]
+
+    def copy(self, slot, kind, way, y, x):
+        block = self.block(slot, kind, self.core)
+        return pltpu.make_async_remote_copy(
+            src_ref=block, dst_ref=block, send_sem=self.sends.at[slot, kind, way],
+            recv_sem=self.receives.at[slot, kind],
+            device_id=(self.p, (y * 4 + x) * 2 + self.core), device_id_type=MESH)
+
+    def along_x(self, slot, kind, way):
+        return self.copy(slot, kind, 1 + way, self.y, (self.x + way) % 4)
+
+    def along_y(self, slot, kind, back):
+        step = self.turn(slot, kind) * (-1 if back else 1)
+        return self.copy(slot, kind, back, (self.y + step + 8) % 8, self.x)
+
+    def turn(self, slot, kind):
+        return self.sign * (1 - 2 * (slot % 2)) if kind == 0 else self.sign
+
+    def across(self, slot, kind, core):
+        block = self.block(slot, kind, core)
+        chip = self.y * 4 + self.x
+        return pltpu.make_async_remote_copy(
+            src_ref=block, dst_ref=block, send_sem=self.over.at[slot, kind - 1],
+            recv_sem=self.came.at[slot, kind - 1],
+            device_id=(self.p, chip * 2 + 1 - self.core), device_id_type=MESH)
+
+    def arrived(self, slot, kind):
+        self.along_x(slot, kind, 1).wait_recv()
+
+    def weights(self, act):
+        act(1)
+
+        @pl.when(self.core == 1)
+        def _():
+            act(2)
+
+    def columns(self):
+        return [(self.x + i) % 4 for i in (0, 1, 3, 2)]
+
+    def spread(self, act, slot, kind):
+        for way in (1, 3, 2):
+            act(self.along_x(slot, kind, way))
+        if kind:
+            act(self.across(slot, kind, self.core))
+
+    def own_sends(self, act):
+        def round_y(kind):
+            act(self.along_y(self.place, kind, 0))
+            act(self.along_y(self.place, kind, 1))
+
+        self.spread(act, self.place, 0)
+        self.weights(round_y)
+        round_y(0)
+        self.weights(lambda kind: self.spread(act, self.place, kind))
+
+    def row_sends(self, act, wait):
+        for column in self.columns()[1:]:
+            slot = (self.y % 4) * 4 + column
+            if wait:
+                self.arrived(slot, 0)
+            act(self.along_y(slot, 0, 0))
+            act(self.along_y(slot, 0, 1))
+
+    def lower_hop(self, act, wait, distance, pair):
+        columns = [(self.x + pair) % 4, (self.x + pair + 2) % 4]
+        for back in range(2 if distance < 4 else 1):
+            step = self.turn(columns[0], 0) * distance * (1 if back else -1)
+            origin = (self.y + step + 8) % 8
+
+            @pl.when(origin // 4 == self.core)
+            def _():
+                for column in columns:
+                    slot = (origin % 4) * 4 + column
+                    if wait:
+                        self.arrived(slot, 0)
+                    if distance < (3 if back else 4):
+                        act(self.along_y(slot, 0, back))
+
+    def weight_hop(self, act, wait, distance):
+        for back in range(2 if distance < 4 else 1):
+            origin = (self.y + self.sign * distance * (1 if back else -1) + 8) % 8
+
+            @pl.when(origin // 4 == self.core)
+            def _():
+                slot = (origin % 4) * 4 + self.x
+
+                def pass_on(kind):
+                    if wait:
+                        self.arrived(slot, kind)
+                    if distance < (3 if back else 4):
+                        act(self.along_y(slot, kind, back))
+                    self.spread(act, slot, kind)
+
+                self.weights(pass_on)
+
+    def weight_across(self, act, wait):
+        for s in range(4):
+            for way in (1, 3, 2):
+                slot = s * 4 + (self.x + way) % 4
+
+                def to_sibling(kind):
+                    if wait:
+                        self.arrived(slot, kind)
+                    act(self.across(slot, kind, self.core))
+
+                self.weights(to_sibling)
+
+    def walk(self, act, wait):
+        @pl.when(self.source)
+        def _():
+            self.own_sends(act)
+            self.row_sends(act, wait)
+
+        self.weight_hop(act, wait, 1)
+        self.lower_hop(act, wait, 1, 0)
+        self.weight_hop(act, wait, 2)
+        self.lower_hop(act, wait, 1, 1)
+        self.weight_hop(act, wait, 3)
+        self.lower_hop(act, wait, 2, 0)
+        self.weight_hop(act, wait, 4)
+        self.lower_hop(act, wait, 2, 1)
+        self.lower_hop(act, wait, 3, 0)
+        self.lower_hop(act, wait, 3, 1)
+        self.weight_across(act, wait)
+        self.lower_hop(act, wait, 4, 0)
+        self.lower_hop(act, wait, 4, 1)
+
+    def run(self):
+        self.walk(lambda copy: copy.start(), True)
+        for slot in range(HALF_CHIPS):
+            self.across(slot, 1, 1 - self.core).wait_recv()
+
+            @pl.when(self.core == 0)
+            def _():
+                self.across(slot, 2, 1 - self.core).wait_recv()
+
+    def finish(self):
+        self.walk(lambda copy: copy.wait_send(), False)
+
+
 def chain(
-    flag_ref, coupled_ref, gram_ref, end_ref, sigma_ref, cross_ref,
-    end_buf, next_buf, next_out, part_out, part_in, part2_out, part2_in, pack, recv, rows_out,
+    flag_ref, weight_hbm, lower_hbm, end_hbm, sigma_ref, cross_ref,
+    weight_rows, lower_rows, end_ref, weight_ref, lower_ref, coupled_ref,
+    rows_there, rows_here, gram_buf, end_buf, next_buf, next_out,
+    part_out, part_in, part2_out, part2_in, pack, recv, rows_out,
+    load_sem, here_sem, ring_send, ring_recv, across_send, across_recv,
     end_sem, next_sem, part_sem, part2_sem, rows_sem, pack_send, pack_recv,
 ):
     parts = 8
@@ -45,11 +201,20 @@
     chip, core = r // 2, r % 2
     half = chip // HALF_CHIPS
     place = chip % HALF_CHIPS
+    y, x = chip // 4, chip % 4
+    source_core = core == half
     sibling = (p, chip * 2 + 1 - core)
 
     def peer(j):
         return (p, (core * HALF_CHIPS + j) * 2 + half)
 
+    loads = [
+        pltpu.make_async_copy(src, dst, load_sem.at[k])
+        for k, (src, dst) in enumerate(
+            ((lower_hbm, lower_rows), (weight_hbm, weight_rows), (end_hbm, end_ref)))
+    ]
+    for load in loads:
+        load.start()
     barrier = pltpu.get_barrier_semaphore()
     pl.semaphore_signal(barrier, 1, device_id=sibling, device_id_type=MESH)
 
@@ -64,15 +229,21 @@
     def is_self(j):
         return jnp.logical_and(core == half, place == j)
 
-    for j in range(HALF_CHIPS):
-        @pl.when(jnp.logical_not(is_self(j)))
-        def _():
-            pl.semaphore_signal(barrier, 1, device_id=peer(j), device_id_type=MESH)
-
-    expected = (
-        1 + jnp.where(p > 0, 1, 0) + jnp.where(p < parts - 1, 1, 0)
-        + HALF_CHIPS - jnp.where(core == half, 1, 0)
-    )
+    for around in (1, 7):
+        there = ((y + around) % 8) * 4 + x
+        pl.semaphore_signal(
+            barrier, 1, device_id=(p, there * 2 + core), device_id_type=MESH)
+    for around in (1, 2, 3):
+        there = y * 4 + (x + around) % 4
+        pl.semaphore_signal(
+            barrier, 1, device_id=(p, there * 2 + core), device_id_type=MESH)
+
+    expected = 6 + jnp.where(p > 0, 1, 0) + jnp.where(p < parts - 1, 1, 0)
+    weight_ref[:HALF_CHIPS, :, HALF:] = jnp.zeros((HALF_CHIPS, PANEL, HALF), BF16)
+    for load in loads:
+        load.wait()
+    rows_here[0] = lower_rows[...].astype(F32)
+    rows_here[1] = weight_rows[...].astype(F32)
     pl.semaphore_wait(barrier, expected)
 
     mine = pl.ds(pl.multiple_of(core * HALF, 128), HALF)
@@ -85,10 +256,48 @@
             src_ref=src, dst_ref=dst, send_sem=sems.at[0], recv_sem=sems.at[1],
             device_id=sibling, device_id_type=MESH)
 
+    here_copy = to_sibling(rows_here, rows_there, here_sem)
+
+    @pl.when(jnp.logical_not(source_core))
+    def _():
+        here_copy.start()
+
     end_copy = to_sibling(end_ref.at[:, theirs], end_buf.at[my_rows], end_sem)
     end_copy.start()
     end_buf[my_rows] = end_ref[:, mine]
-    end_copy.wait()
+    ring = Ring(
+        lower_ref, weight_ref, (ring_send, ring_recv, across_send, across_recv),
+        p, y, x, core, place, source_core)
+
+    @pl.when(source_core)
+    def _():
+        here_copy.wait_recv()
+        for which, there in ((0, rows_there[0]), (1, rows_there[1])):
+            ours = rows_here[which]
+            low = jnp.where(core == 0, ours, there)
+            high = jnp.where(core == 0, there, ours)
+            both = jnp.concatenate([low, high], axis=0).astype(BF16)
+            if which == 0:
+                lower_ref[place] = both
+            else:
+                weight_ref[chip] = both
+
+    ring.run()
+
+    @pl.loop(0, B // WINDOW)
+    def _(k):
+        columns = pl.ds(pl.multiple_of(k * WINDOW, WINDOW), WINDOW)
+        right = weight_ref[HALF_CHIPS:, :, columns].reshape(HALF, WINDOW)
+        total = dot(lower_ref[:, :, HALF:].reshape(HALF, HALF), right)
+        coupled_ref[:, :, columns] = total.astype(BF16).reshape(HALF_CHIPS, PANEL, WINDOW)
+
+        @pl.when(k < HALF // WINDOW)
+        def _():
+            left = weight_ref[:HALF_CHIPS, :, columns].reshape(HALF, WINDOW)
+            more = dot(lower_ref[:, :, :HALF].reshape(HALF, HALF), left) + total
+            coupled_ref[:, :, columns] = more.astype(BF16).reshape(HALF_CHIPS, PANEL, WINDOW)
+
+    end_copy.wait_recv()
 
     next_copy = pltpu.make_async_remote_copy(
         src_ref=next_out, dst_ref=next_buf, send_sem=next_sem.at[0], recv_sem=next_sem.at[1],
@@ -102,7 +311,7 @@
     def _():
         next_buf[...] = jnp.zeros_like(next_buf)
 
-    use_end = jnp.logical_or(flag_ref[0] == 1, p == parts - 1)
+    use_end = jnp.logical_or(flag_ref[p] == 1, p == parts - 1)
     source = jnp.where(use_end, end_buf[...].astype(BF16), next_buf[...])
 
     part_copy = to_sibling(part_out, part_in, part_sem)
@@ -138,6 +347,14 @@
     cross_copy.start()
     cross_ref[:, mine] = rows_out[0, my_rows]
 
+    window = jnp.minimum(chip * PANEL // 128, (B - WINDOW) // 128) * 128
+    chips = pl.ds(core * HALF_CHIPS, HALF_CHIPS)
+    own = weight_ref[chips, :, pl.ds(pl.multiple_of(window, 128), WINDOW)].reshape(HALF, WINDOW).T
+    for k in range(B // WINDOW):
+        gram_buf[:, WINDOW * k:WINDOW * (k + 1)] = dot(
+            own, weight_ref[chips, :, WINDOW * k:WINDOW * (k + 1)].reshape(HALF, WINDOW))
+    gram_rows = pl.ds(pl.multiple_of(chip * PANEL - window, 16), PANEL)
+
     for j in range(HALF_CHIPS):
         @pl.when(jnp.logical_not(is_self(j)))
         def _():
@@ -149,12 +366,14 @@
     def update(columns):
         def rows(k):
             return coupled_ref[:, 16 * k:16 * k + 16, columns].reshape(HALF_CHIPS * 16, HALF)
-        return dot(first[:48], rows(0)) + dot(first[64:112], rows(1)) + dot(second[:48], rows(2))
+        return (
+            gram_buf[gram_rows, columns]
+            + dot(first[:48], rows(0)) + dot(first[64:112], rows(1)) + dot(second[:48], rows(2)))
 
     part2_copy = to_sibling(part2_out, part2_in, part2_sem)
     part2_out[...] = update(theirs)
     part2_copy.start()
-    sigma = update(mine) + gram_ref[...]
+    sigma = update(mine)
     part2_copy.wait_recv()
     sigma = sigma + part2_in[...]
 
@@ -172,6 +391,13 @@
     def _():
         next_copy.wait_send()
 
+    end_copy.wait_send()
+
+    @pl.when(jnp.logical_not(source_core))
+    def _():
+        here_copy.wait_send()
+
+    ring.finish()
     part_copy.wait_send()
     part2_copy.wait_send()
     for j in range(HALF_CHIPS):
@@ -182,15 +408,24 @@
     sigma_copy.wait()
 
 
-def run_chain(flag, coupled, gram, end):
+def run_chain(flag, weight, lower, end):
     vmem = pl.BlockSpec(memory_space=pltpu.VMEM)
     dma = pltpu.SemaphoreType.DMA
     return pl.pallas_call(
         chain,
         out_shape=[jax.ShapeDtypeStruct((OWN, B), F32)] * 2,
-        in_specs=[pl.BlockSpec(memory_space=pltpu.SMEM), vmem, vmem, vmem],
+        in_specs=[pl.BlockSpec(memory_space=pltpu.SMEM)] + [pl.BlockSpec(memory_space=pl.ANY)] * 3,
         out_specs=[vmem, vmem],
         scratch_shapes=[
+            pltpu.VMEM((OWN, B), BF16),
+            pltpu.VMEM((OWN, B), BF16),
+            pltpu.VMEM((OWN, B), F32),
+            pltpu.VMEM((CHIPS, PANEL, B), BF16),
+            pltpu.VMEM((HALF_CHIPS, PANEL, B), BF16),
+            pltpu.VMEM((HALF_CHIPS, PANEL, B), BF16),
+            pltpu.VMEM((2, OWN, B), F32),
+            pltpu.VMEM((2, OWN, B), F32),
+            pltpu.VMEM((WINDOW, B), F32),
             pltpu.VMEM((PANEL, HALF), F32),
             pltpu.VMEM((PANEL, HALF), BF16),
             pltpu.VMEM((PANEL, HALF), BF16),
@@ -201,29 +436,19 @@
             pltpu.VMEM((HALF_CHIPS, 32, 128), BF16),
             pltpu.VMEM((HALF_CHIPS, 32, 128), BF16),
             pltpu.VMEM((2, PANEL, HALF), F32),
+            dma((3,)), dma((2,)),
+            dma((HALF_CHIPS, 3, 5)), dma((HALF_CHIPS, 3)),
+            dma((HALF_CHIPS, 2)), dma((HALF_CHIPS, 2)),
             dma((2,)), dma((2,)), dma((2,)), dma((2,)), dma((2, 2)),
             dma((HALF_CHIPS,)), dma((HALF_CHIPS,)),
         ],
         compiler_params=pltpu.CompilerParams(
             collective_id=0, has_side_effects=True, vmem_limit_bytes=40 * 1024 * 1024),
-    )(flag, coupled, gram, end)
+    )(flag, weight, lower, end)
 
 
 def shards(w_inv, lower_block, sigma_end, chain_break):
-    weight_rows = w_inv[0]
-    lower_rows = lower_block[0]
-    r = lax.axis_index("rows")
-    chip, core = r // 2, r % 2
-    weight_full = lax.all_gather(weight_rows, "rows", axis=0, tiled=True)
-    coupled_rows = jnp.dot(lower_rows, weight_full, preferred_element_type=F32)
-    coupled_full = lax.all_gather(coupled_rows.astype(BF16), "rows", axis=0, tiled=True)
-    coupled = lax.dynamic_slice_in_dim(coupled_full, core * HALF, HALF, 0)
-    own = lax.dynamic_slice_in_dim(weight_full, chip * PANEL, PANEL, 1)
-    cols = lax.dynamic_slice_in_dim(weight_full, core * HALF, HALF, 1)
-    gram = lax.dot_general(own, cols, (((0,), (0,)), ((), ())), preferred_element_type=F32)
-    part = lax.axis_index("tm")
-    flag = lax.dynamic_slice_in_dim(chain_break, part, 1, 0)
-    sigma, cross = run_chain(flag, coupled.reshape(HALF_CHIPS, PANEL, B), gram, sigma_end)
+    sigma, cross = run_chain(chain_break, w_inv[0], lower_block[0], sigma_end)
     return (sigma[None], cross[None])
 
 

time: 317 us -> 174 us (0.55)
  waiting for transfers between devices: 174 us -> 0 us
  Pallas kernels: 117 us -> 169 us
  between operations: 14.1 us -> 0.65 us
  matrix products: 6.27 us -> 0 us
    all_gather x2 -> x0, waiting for transfers between devices: 173 us -> none  [the longest x1 93.9 us: shards(): weight_full = lax.all_gather(weight_rows, 'rows', axis=0, tiled=True)]
    pallas_call x1, Pallas kernels: 117 us -> 169 us  [run_chain(): pl.pallas_call(chain, out_shape=[jax.ShapeDtypeStruct((OWN, B), F32)] * 2...]
    dot_general x2 -> x0, matrix products: 6.27 us -> none  [the longest x1 3.71 us: shards(): coupled_rows = jnp.dot(lower_rows, weight_full, preferred_element_type=F32)]
    unnamed x8 -> x10, local copies, waits for them, and re-layouts: 1.34 us -> 4.65 us
  transfers between devices with their start and end apart: 2 -> 0, of which waited for: 2 -> 0; matrix products, arithmetic and copies ran while one was open for 1% -> 0% of each run, Pallas kernels for 0% -> 0%
where the time goes in v3:
time: 174 us
  Pallas kernels  169 us (97%)
  local copies, waits for them, and re-layouts  4.65 us (3%)
    pallas_call x1, Pallas kernels, run_chain(): pl.pallas_call(chain, out_shape=[jax.ShapeDtypeStruct((OWN, B), F32)] * 2...  169 us
    unnamed x10, local copies, waits for them, and re-layouts  4.65 us

profile of v3, /device:TPU:1, one launch (start us, length us, event | category | flops | bytes accessed | tf_op | source)
XLA Modules:
  0.0 174.0 jit_solution(9698005414270446173)
XLA Ops:
  0.6 0.0 copy-start.3
  0.6 0.6 copy-done.3
  1.3 0.0 copy-start
  1.3 0.9 copy-done
  2.2 0.0 copy-start.1
  2.2 0.9 copy-done.1
  3.1 0.0 copy-start.2
  3.1 0.9 copy-done.2
  4.0 168.7 %shard_map.59 = (f32[24,1536]{1,0:T(8,128)S(1)}, f32[24,1536]{1,0:T(8,128)S(1)}) custom-call(s32[8]{0:T(128)S(1)} %copy-done.3, bf16[24,1536]{1,0:T(8,128)(2,1)S(1)} %bitcast.6, bf16[24,1536]{1,0:T(8,128)(2,1)S(1)} %bitcast.7, f32[24,1536]{1,0:T(8,128)S(1)} %copy-done), custom_call_target="tpu_custom_call" | custom-call | tf_op jit(solution)/shard_map/pallas_call | solution.py:414
  172.7 0.7 copy.8
  173.3 0.7 copy.9
Async XLA Ops:
  0.6 0.7 copy-start.3
  1.3 0.9 copy-start
  2.2 0.9 copy-start.1
  3.1 0.9 copy-start.2

commit v4 on v3

--- a/solution.py
+++ b/solution.py
@@ -15,6 +15,7 @@
 OWN = 24
 HALF = 768
 WINDOW = 256
+SPLIT = 4
 
 
 def dot(a, b):
@@ -187,12 +188,38 @@
         self.walk(lambda copy: copy.wait_send(), False)
 
 
+class PlainRing(Ring):
+    def __init__(self, held, sems, p, y, x, core, place, source):
+        super().__init__(held, held, sems + (None, None), p, y, x, core, place, source)
+
+    def block(self, slot, kind, core):
+        return self.lower.at[slot, :, HALF * kind:HALF * (kind + 1)]
+
+    def weights(self, act):
+        act(1)
+
+    def spread(self, act, slot, kind):
+        for way in (1, 3, 2):
+            act(self.along_x(slot, kind, way))
+
+    def weight_across(self, act, wait):
+        if wait:
+            for s in range(4):
+                for way in (1, 3, 2):
+                    self.arrived(s * 4 + (self.x + way) % 4, 1)
+
+    def run(self):
+        self.walk(lambda copy: copy.start(), True)
+
+
 def chain(
     flag_ref, weight_hbm, lower_hbm, end_hbm, sigma_ref, cross_ref,
     weight_rows, lower_rows, end_ref, weight_ref, lower_ref, coupled_ref,
+    through_ref, through_in, through_out, first_sigma,
     rows_there, rows_here, gram_buf, end_buf, next_buf, next_out,
     part_out, part_in, part2_out, part2_in, pack, recv, rows_out,
     load_sem, here_sem, ring_send, ring_recv, across_send, across_recv,
+    through_send, through_recv, through_sem, through_hop, ahead_sem,
     end_sem, next_sem, part_sem, part2_sem, rows_sem, pack_send, pack_recv,
 ):
     parts = 8
@@ -238,7 +265,13 @@
         pl.semaphore_signal(
             barrier, 1, device_id=(p, there * 2 + core), device_id_type=MESH)
 
-    expected = 6 + jnp.where(p > 0, 1, 0) + jnp.where(p < parts - 1, 1, 0)
+    @pl.when(p < SPLIT - 1)
+    def _():
+        pl.semaphore_signal(barrier, 1, device_id=(SPLIT, r), device_id_type=MESH)
+
+    expected = (
+        6 + jnp.where(p > 0, 1, 0) + jnp.where(p < parts - 1, 1, 0)
+        + jnp.where(p == SPLIT, SPLIT - 1, 0))
     weight_ref[:HALF_CHIPS, :, HALF:] = jnp.zeros((HALF_CHIPS, PANEL, HALF), BF16)
     for load in loads:
         load.wait()
@@ -298,98 +331,221 @@
             coupled_ref[:, :, columns] = more.astype(BF16).reshape(HALF_CHIPS, PANEL, WINDOW)
 
     end_copy.wait_recv()
-
-    next_copy = pltpu.make_async_remote_copy(
-        src_ref=next_out, dst_ref=next_buf, send_sem=next_sem.at[0], recv_sem=next_sem.at[1],
-        device_id=(jnp.maximum(p - 1, 0), r), device_id_type=MESH)
-
-    @pl.when(p < parts - 1)
-    def _():
-        next_copy.wait_recv()
-
-    @pl.when(p == parts - 1)
-    def _():
-        next_buf[...] = jnp.zeros_like(next_buf)
-
-    use_end = jnp.logical_or(flag_ref[p] == 1, p == parts - 1)
-    source = jnp.where(use_end, end_buf[...].astype(BF16), next_buf[...])
-
-    part_copy = to_sibling(part_out, part_in, part_sem)
-    part_out[...] = dot(source, coupled_ref[:, :, theirs].reshape(HALF, HALF))
-    part_copy.start()
-    product = dot(source, coupled_ref[:, :, mine].reshape(HALF, HALF))
-    part_copy.wait_recv()
-    product = product + part_in[...]
-
-    def pack_copy(j):
+    end_b = end_buf[...].astype(BF16)
+    broken = flag_ref[p] == 1
+    early = p < SPLIT
+
+    def down(src, dst, send, receive, target):
         return pltpu.make_async_remote_copy(
-            src_ref=pack.at[j], dst_ref=recv.at[place], send_sem=pack_send.at[j],
-            recv_sem=pack_recv.at[place], device_id=peer(j), device_id_type=MESH)
-
-    def arrival(j):
+            src_ref=src, dst_ref=dst, send_sem=send, recv_sem=receive,
+            device_id=(target, r), device_id_type=MESH)
+
+    below = jnp.maximum(p - 1, 0)
+    hops = [
+        down(next_out.at[0], next_buf.at[0], next_sem.at[0, 0], next_sem.at[0, 1], below),
+        None,
+        down(next_out.at[1], next_buf.at[2], next_sem.at[2, 0], next_sem.at[2, 1], below),
+    ]
+    jumps = [
+        down(next_out.at[0], next_buf.at[1], ahead_sem.at[q], next_sem.at[1, 1], q)
+        for q in range(SPLIT)
+    ]
+    through_copy = down(
+        through_out, through_in, through_hop.at[0], through_hop.at[1], below)
+
+    def sum_halves(k, source, right_ref):
+        copy = to_sibling(part_out.at[k], part_in.at[k], part_sem.at[k])
+        part_out[k] = dot(source, right_ref[:, :, theirs].reshape(HALF, HALF))
+        copy.start()
+        own = dot(source, right_ref[:, :, mine].reshape(HALF, HALF))
+        copy.wait_recv()
+        return own + part_in[k]
+
+    def pack_copy(k, j):
         return pltpu.make_async_remote_copy(
-            src_ref=pack.at[j], dst_ref=recv.at[j], send_sem=pack_send.at[j],
-            recv_sem=pack_recv.at[j], device_id=peer(j), device_id_type=MESH)
-
-    for j in range(HALF_CHIPS):
-        pack[j] = message(product, j)
-
-        @pl.when(jnp.logical_not(is_self(j)))
-        def _():
-            pack_copy(j).start()
-
-        @pl.when(is_self(j))
-        def _():
-            recv[j] = pack[j]
-
-    rows_out[0] = -product
-    cross_copy = to_sibling(rows_out.at[0, their_rows], cross_ref.at[:, mine], rows_sem.at[0])
-    cross_copy.start()
-    cross_ref[:, mine] = rows_out[0, my_rows]
-
-    window = jnp.minimum(chip * PANEL // 128, (B - WINDOW) // 128) * 128
-    chips = pl.ds(core * HALF_CHIPS, HALF_CHIPS)
-    own = weight_ref[chips, :, pl.ds(pl.multiple_of(window, 128), WINDOW)].reshape(HALF, WINDOW).T
-    for k in range(B // WINDOW):
-        gram_buf[:, WINDOW * k:WINDOW * (k + 1)] = dot(
-            own, weight_ref[chips, :, WINDOW * k:WINDOW * (k + 1)].reshape(HALF, WINDOW))
-    gram_rows = pl.ds(pl.multiple_of(chip * PANEL - window, 16), PANEL)
-
-    for j in range(HALF_CHIPS):
-        @pl.when(jnp.logical_not(is_self(j)))
-        def _():
-            arrival(j).wait_recv()
-
-    first = recv[:, :16].reshape(HALF_CHIPS * 16, 128).T
-    second = recv[:, 16:].reshape(HALF_CHIPS * 16, 128).T
-
-    def update(columns):
-        def rows(k):
-            return coupled_ref[:, 16 * k:16 * k + 16, columns].reshape(HALF_CHIPS * 16, HALF)
-        return (
-            gram_buf[gram_rows, columns]
-            + dot(first[:48], rows(0)) + dot(first[64:112], rows(1)) + dot(second[:48], rows(2)))
-
-    part2_copy = to_sibling(part2_out, part2_in, part2_sem)
-    part2_out[...] = update(theirs)
-    part2_copy.start()
-    sigma = update(mine)
-    part2_copy.wait_recv()
-    sigma = sigma + part2_in[...]
-
-    @pl.when(p > 0)
-    def _():
-        next_out[...] = sigma.astype(BF16)
-        next_copy.start()
-
-    rows_out[1] = sigma
-    sigma_copy = to_sibling(rows_out.at[1, their_rows], sigma_ref.at[:, mine], rows_sem.at[1])
-    sigma_copy.start()
-    sigma_ref[:, mine] = rows_out[1, my_rows]
-
-    @pl.when(p > 0)
-    def _():
-        next_copy.wait_send()
+            src_ref=pack.at[k, j], dst_ref=recv.at[k, place], send_sem=pack_send.at[k, j],
+            recv_sem=pack_recv.at[k, place], device_id=peer(j), device_id_type=MESH)
+
+    def arrival(k, j):
+        return pltpu.make_async_remote_copy(
+            src_ref=pack.at[k, j], dst_ref=recv.at[k, j], send_sem=pack_send.at[k, j],
+            recv_sem=pack_recv.at[k, j], device_id=peer(j), device_id_type=MESH)
+
+    def emit(which, value, out_ref, act):
+        copy = to_sibling(
+            rows_out.at[which, their_rows], out_ref.at[:, mine], rows_sem.at[which])
+        if act == "start":
+            rows_out[which] = value
+            copy.start()
+            out_ref[:, mine] = rows_out[which, my_rows]
+        else:
+            copy.wait()
+
+    def step(k, source, right_ref, meanwhile):
+        product = sum_halves(k, source, right_ref)
+        for j in range(HALF_CHIPS):
+            pack[k, j] = message(product, j)
+
+            @pl.when(jnp.logical_not(is_self(j)))
+            def _():
+                pack_copy(k, j).start()
+
+            @pl.when(is_self(j))
+            def _():
+                recv[k, j] = pack[k, j]
+
+        base = meanwhile(product)
+        for j in range(HALF_CHIPS):
+            @pl.when(jnp.logical_not(is_self(j)))
+            def _():
+                arrival(k, j).wait_recv()
+
+        first = recv[k, :, :16].reshape(HALF_CHIPS * 16, 128).T
+        second = recv[k, :, 16:].reshape(HALF_CHIPS * 16, 128).T
+
+        def update(columns):
+            def rows(i):
+                return right_ref[:, 16 * i:16 * i + 16, columns].reshape(HALF_CHIPS * 16, HALF)
+            total = dot(first[:48], rows(0)) + dot(first[64:112], rows(1))
+            total = total + dot(second[:48], rows(2))
+            return total if base is None else total + base(columns)
+
+        copy = to_sibling(part2_out.at[k], part2_in.at[k], part2_sem.at[k])
+        part2_out[k] = update(theirs)
+        copy.start()
+        sigma = update(mine)
+        copy.wait_recv()
+        return sigma + part2_in[k]
+
+    through_ring = PlainRing(
+        through_ref, (through_send, through_recv), p, y, x, core, place, source_core)
+    through_half = to_sibling(through_out, through_out, through_sem.at[0])
+    through_here = to_sibling(through_out, through_ref.at[place, :, mine], through_sem.at[1])
+    zero = jnp.zeros((PANEL, HALF), BF16)
+
+    @pl.when(p == SPLIT - 1)
+    def _():
+        @pl.when(source_core)
+        def _():
+            next_out[1] = jnp.where(broken, zero, coupled_ref[place, :, theirs])
+            half_copy = to_sibling(next_out.at[1], through_out, through_sem.at[0])
+            half_copy.start()
+            through_out[...] = jnp.where(broken, zero, coupled_ref[place, :, mine])
+            half_copy.wait_send()
+
+        @pl.when(jnp.logical_not(source_core))
+        def _():
+            through_half.wait_recv()
+
+        through_copy.start()
+
+        @pl.loop(0, HALF_CHIPS)
+        def _(j):
+            rows = coupled_ref[j]
+            through_ref[j] = jnp.where(broken, jnp.zeros_like(rows), rows)
+
+    @pl.when(p < SPLIT - 1)
+    def _():
+        through_copy.wait_recv()
+        rows = sum_halves(2, through_in[...], coupled_ref).astype(BF16)
+        through_out[...] = jnp.where(broken, zero, rows)
+
+        @pl.when(p > 0)
+        def _():
+            through_copy.start()
+
+        @pl.when(source_core)
+        def _():
+            through_ref[place, :, mine] = through_out[...]
+
+        @pl.when(jnp.logical_not(source_core))
+        def _():
+            through_here.start()
+
+    def gather_through():
+        @pl.when(source_core)
+        def _():
+            to_sibling(through_out, through_ref.at[place, :, theirs], through_sem.at[1]).wait_recv()
+
+        through_ring.run()
+
+    @pl.when(p < SPLIT - 2)
+    def _():
+        gather_through()
+
+    has_above = jnp.logical_and(p != parts - 1, p != SPLIT - 1)
+
+    @pl.when(has_above)
+    def _():
+        hops[0].wait_recv()
+
+    @pl.when(jnp.logical_not(has_above))
+    def _():
+        next_buf[0] = zero
+
+    use_end = jnp.logical_or(broken, p == parts - 1)
+
+    def gram(product):
+        window = jnp.minimum(chip * PANEL // 128, (B - WINDOW) // 128) * 128
+        chips = pl.ds(core * HALF_CHIPS, HALF_CHIPS)
+        own = weight_ref[chips, :, pl.ds(pl.multiple_of(window, 128), WINDOW)]
+        own = own.reshape(HALF, WINDOW).T
+        for k in range(B // WINDOW):
+            columns = slice(WINDOW * k, WINDOW * (k + 1))
+            gram_buf[:, columns] = dot(own, weight_ref[chips, :, columns].reshape(HALF, WINDOW))
+        gram_rows = pl.ds(pl.multiple_of(chip * PANEL - window, 16), PANEL)
+
+        @pl.when(jnp.logical_not(early))
+        def _():
+            emit(0, -product, cross_ref, "start")
+
+        return lambda columns: gram_buf[gram_rows, columns]
+
+    sigma = step(0, jnp.where(use_end, end_b, next_buf[0]), coupled_ref, gram)
+    next_out[0] = sigma.astype(BF16)
+    sends_down = jnp.logical_and(p > 0, p != SPLIT)
+
+    @pl.when(sends_down)
+    def _():
+        hops[0].start()
+
+    @pl.when(p == SPLIT)
+    def _():
+        for jump in jumps:
+            jump.start()
+
+    @pl.when(jnp.logical_not(early))
+    def _():
+        emit(1, sigma, sigma_ref, "start")
+
+    @pl.when(early)
+    def _():
+        first_sigma[...] = sigma
+
+        @pl.when(p == SPLIT - 2)
+        def _():
+            gather_through()
+
+        jumps[0].wait_recv()
+        whole = first_sigma[...] + step(1, next_buf[1], through_ref, lambda product: None)
+        next_out[1] = whole.astype(BF16)
+
+        @pl.when(p > 0)
+        def _():
+            hops[2].start()
+
+        emit(1, whole, sigma_ref, "start")
+
+        @pl.when(p < SPLIT - 1)
+        def _():
+            hops[2].wait_recv()
+
+        @pl.when(p == SPLIT - 1)
+        def _():
+            next_buf[2] = next_buf[1]
+
+        source = jnp.where(broken, end_b, next_buf[2])
+        emit(0, -sum_halves(3, source, coupled_ref), cross_ref, "start")
 
     end_copy.wait_send()
 
@@ -398,14 +554,50 @@
         here_copy.wait_send()
 
     ring.finish()
-    part_copy.wait_send()
-    part2_copy.wait_send()
-    for j in range(HALF_CHIPS):
-        @pl.when(jnp.logical_not(is_self(j)))
-        def _():
-            pack_copy(j).wait_send()
-    cross_copy.wait()
-    sigma_copy.wait()
+
+    def sent(k):
+        to_sibling(part_out.at[k], part_in.at[k], part_sem.at[k]).wait_send()
+
+    def step_sent(k):
+        sent(k)
+        to_sibling(part2_out.at[k], part2_in.at[k], part2_sem.at[k]).wait_send()
+        for j in range(HALF_CHIPS):
+            @pl.when(jnp.logical_not(is_self(j)))
+            def _():
+                pack_copy(k, j).wait_send()
+
+    step_sent(0)
+
+    @pl.when(sends_down)
+    def _():
+        hops[0].wait_send()
+
+    @pl.when(p == SPLIT)
+    def _():
+        for jump in jumps:
+            jump.wait_send()
+
+    @pl.when(early)
+    def _():
+        step_sent(1)
+        sent(3)
+
+        @pl.when(p > 0)
+        def _():
+            through_copy.wait_send()
+            hops[2].wait_send()
+
+    @pl.when(p < SPLIT - 1)
+    def _():
+        sent(2)
+        through_ring.finish()
+
+        @pl.when(jnp.logical_not(source_core))
+        def _():
+            through_here.wait_send()
+
+    emit(0, None, cross_ref, "wait")
+    emit(1, None, sigma_ref, "wait")
 
 
 def run_chain(flag, weight, lower, end):
@@ -423,24 +615,30 @@
             pltpu.VMEM((CHIPS, PANEL, B), BF16),
             pltpu.VMEM((HALF_CHIPS, PANEL, B), BF16),
             pltpu.VMEM((HALF_CHIPS, PANEL, B), BF16),
+            pltpu.VMEM((HALF_CHIPS, PANEL, B), BF16),
+            pltpu.VMEM((PANEL, HALF), BF16),
+            pltpu.VMEM((PANEL, HALF), BF16),
+            pltpu.VMEM((PANEL, HALF), F32),
             pltpu.VMEM((2, OWN, B), F32),
             pltpu.VMEM((2, OWN, B), F32),
             pltpu.VMEM((WINDOW, B), F32),
             pltpu.VMEM((PANEL, HALF), F32),
-            pltpu.VMEM((PANEL, HALF), BF16),
-            pltpu.VMEM((PANEL, HALF), BF16),
-            pltpu.VMEM((PANEL, HALF), F32),
-            pltpu.VMEM((PANEL, HALF), F32),
-            pltpu.VMEM((PANEL, HALF), F32),
-            pltpu.VMEM((PANEL, HALF), F32),
-            pltpu.VMEM((HALF_CHIPS, 32, 128), BF16),
-            pltpu.VMEM((HALF_CHIPS, 32, 128), BF16),
+            pltpu.VMEM((3, PANEL, HALF), BF16),
+            pltpu.VMEM((2, PANEL, HALF), BF16),
+            pltpu.VMEM((4, PANEL, HALF), F32),
+            pltpu.VMEM((4, PANEL, HALF), F32),
+            pltpu.VMEM((2, PANEL, HALF), F32),
+            pltpu.VMEM((2, PANEL, HALF), F32),
+            pltpu.VMEM((2, HALF_CHIPS, 32, 128), BF16),
+            pltpu.VMEM((2, HALF_CHIPS, 32, 128), BF16),
             pltpu.VMEM((2, PANEL, HALF), F32),
             dma((3,)), dma((2,)),
             dma((HALF_CHIPS, 3, 5)), dma((HALF_CHIPS, 3)),
             dma((HALF_CHIPS, 2)), dma((HALF_CHIPS, 2)),
-            dma((2,)), dma((2,)), dma((2,)), dma((2,)), dma((2, 2)),
-            dma((HALF_CHIPS,)), dma((HALF_CHIPS,)),
+            dma((HALF_CHIPS, 2, 5)), dma((HALF_CHIPS, 2)),
+            dma((2, 2)), dma((2,)), dma((SPLIT,)),
+            dma((2,)), dma((3, 2)), dma((4, 2)), dma((2, 2)), dma((2, 2)),
+            dma((2, HALF_CHIPS)), dma((2, HALF_CHIPS)),
         ],
         compiler_params=pltpu.CompilerParams(
             collective_id=0, has_side_effects=True, vmem_limit_bytes=40 * 1024 * 1024),

time: 174 us -> 141 us (0.81)
  Pallas kernels: 169 us -> 135 us
    pallas_call x1, Pallas kernels: 169 us -> 135 us  [run_chain(): pl.pallas_call(chain, out_shape=[jax.ShapeDtypeStruct((OWN, B), F32)] * 2...]
where the time goes in v4:
time: 141 us
  Pallas kernels  135 us (96%)
  local copies, waits for them, and re-layouts  4.65 us (3%)
    pallas_call x1, Pallas kernels, run_chain(): pl.pallas_call(chain, out_shape=[jax.ShapeDtypeStruct((OWN, B), F32)] * 2...  135 us
    unnamed x10, local copies, waits for them, and re-layouts  4.65 us

profile of v4, /device:TPU:1, one launch (start us, length us, event | category | flops | bytes accessed | tf_op | source)
XLA Modules:
  0.0 140.6 jit_solution(10598251264178502515)
XLA Ops:
  0.6 0.0 copy-start.3
  0.6 0.6 copy-done.3
  1.3 0.0 copy-start
  1.3 0.9 copy-done
  2.2 0.0 copy-start.1
  2.2 0.9 copy-done.1
  3.1 0.0 copy-start.2
  3.1 0.9 copy-done.2
  4.0 135.3 %shard_map.59 = (f32[24,1536]{1,0:T(8,128)S(1)}, f32[24,1536]{1,0:T(8,128)S(1)}) custom-call(s32[8]{0:T(128)S(1)} %copy-done.3, bf16[24,1536]{1,0:T(8,128)(2,1)S(1)} %bitcast.6, bf16[24,1536]{1,0:T(8,128)(2,1)S(1)} %bitcast.7, f32[24,1536]{1,0:T(8,128)S(1)} %copy-done), custom_call_target="tpu_custom_call" | custom-call | tf_op jit(solution)/shard_map/pallas_call | solution.py:606
  139.3 0.7 copy.8
  140.0 0.7 copy.9
Async XLA Ops:
  0.6 0.7 copy-start.3
  1.3 0.9 copy-start
  2.2 0.9 copy-start.1
  3.1 0.9 copy-start.2

commit v5 on v4

--- a/solution.py
+++ b/solution.py
@@ -39,7 +39,7 @@
 class Ring:
     def __init__(self, lower, weight, sems, p, y, x, core, place, source):
         self.lower, self.weight = lower, weight
-        self.sends, self.receives, self.over, self.came = sems
+        self.sends, self.receives, self.over = sems
         self.p, self.y, self.x, self.core = p, y, x, core
         self.place, self.source = place, source
         self.sign = 1 - 2 * core
@@ -52,9 +52,14 @@
     def copy(self, slot, kind, way, y, x):
         block = self.block(slot, kind, self.core)
         return pltpu.make_async_remote_copy(
-            src_ref=block, dst_ref=block, send_sem=self.sends.at[slot, kind, way],
+            src_ref=block, dst_ref=block, send_sem=self.sends.at[self.sender(slot, kind, way)],
             recv_sem=self.receives.at[slot, kind],
             device_id=(self.p, (y * 4 + x) * 2 + self.core), device_id_type=MESH)
+
+    def sender(self, slot, kind, way):
+        if kind:
+            return 35 + 20 * (kind - 1) + 5 * (slot // 4) + way
+        return 2 * slot + way if way < 2 else 30 + way
 
     def along_x(self, slot, kind, way):
         return self.copy(slot, kind, 1 + way, self.y, (self.x + way) % 4)
@@ -66,12 +71,10 @@
     def turn(self, slot, kind):
         return self.sign * (1 - 2 * (slot % 2)) if kind == 0 else self.sign
 
-    def across(self, slot, kind, core):
-        block = self.block(slot, kind, core)
+    def across(self, block):
         chip = self.y * 4 + self.x
         return pltpu.make_async_remote_copy(
-            src_ref=block, dst_ref=block, send_sem=self.over.at[slot, kind - 1],
-            recv_sem=self.came.at[slot, kind - 1],
+            src_ref=block, dst_ref=block, send_sem=self.over.at[0], recv_sem=self.over.at[1],
             device_id=(self.p, chip * 2 + 1 - self.core), device_id_type=MESH)
 
     def arrived(self, slot, kind):
@@ -87,21 +90,21 @@
     def columns(self):
         return [(self.x + i) % 4 for i in (0, 1, 3, 2)]
 
-    def spread(self, act, slot, kind):
+    def spread(self, act, slot, kind, first):
         for way in (1, 3, 2):
             act(self.along_x(slot, kind, way))
-        if kind:
-            act(self.across(slot, kind, self.core))
-
-    def own_sends(self, act):
+        if kind and first:
+            self.across(self.block(slot, kind, self.core)).start()
+
+    def own_sends(self, act, first):
         def round_y(kind):
             act(self.along_y(self.place, kind, 0))
             act(self.along_y(self.place, kind, 1))
 
-        self.spread(act, self.place, 0)
+        self.spread(act, self.place, 0, first)
         self.weights(round_y)
         round_y(0)
-        self.weights(lambda kind: self.spread(act, self.place, kind))
+        self.weights(lambda kind: self.spread(act, self.place, kind, first))
 
     def row_sends(self, act, wait):
         for column in self.columns()[1:]:
@@ -139,26 +142,37 @@
                         self.arrived(slot, kind)
                     if distance < (3 if back else 4):
                         act(self.along_y(slot, kind, back))
-                    self.spread(act, slot, kind)
+                    self.spread(act, slot, kind, wait)
 
                 self.weights(pass_on)
 
-    def weight_across(self, act, wait):
+    def weight_across(self):
         for s in range(4):
             for way in (1, 3, 2):
                 slot = s * 4 + (self.x + way) % 4
 
                 def to_sibling(kind):
-                    if wait:
-                        self.arrived(slot, kind)
-                    act(self.across(slot, kind, self.core))
+                    self.arrived(slot, kind)
+                    self.across(self.block(slot, kind, self.core)).start()
 
                 self.weights(to_sibling)
+
+    def both_ways(self, act):
+        lower_rows = self.weight.at[:HALF_CHIPS, :, :HALF]
+        upper_rows = self.weight.at[HALF_CHIPS:]
+
+        @pl.when(self.core == 0)
+        def _():
+            act(self.across(lower_rows), self.across(upper_rows))
+
+        @pl.when(self.core == 1)
+        def _():
+            act(self.across(upper_rows), self.across(lower_rows))
 
     def walk(self, act, wait):
         @pl.when(self.source)
         def _():
-            self.own_sends(act)
+            self.own_sends(act, wait)
             self.row_sends(act, wait)
 
         self.weight_hop(act, wait, 1)
@@ -171,18 +185,13 @@
         self.lower_hop(act, wait, 2, 1)
         self.lower_hop(act, wait, 3, 0)
         self.lower_hop(act, wait, 3, 1)
-        self.weight_across(act, wait)
-        self.lower_hop(act, wait, 4, 0)
-        self.lower_hop(act, wait, 4, 1)
-
-    def run(self):
+
+    def run(self, arrived):
         self.walk(lambda copy: copy.start(), True)
-        for slot in range(HALF_CHIPS):
-            self.across(slot, 1, 1 - self.core).wait_recv()
-
-            @pl.when(self.core == 0)
-            def _():
-                self.across(slot, 2, 1 - self.core).wait_recv()
+        self.weight_across()
+        arrived()
+        self.lower_hop(None, True, 4, 0)
+        self.lower_hop(None, True, 4, 1)
 
     def finish(self):
         self.walk(lambda copy: copy.wait_send(), False)
@@ -190,7 +199,7 @@
 
 class PlainRing(Ring):
     def __init__(self, held, sems, p, y, x, core, place, source):
-        super().__init__(held, held, sems + (None, None), p, y, x, core, place, source)
+        super().__init__(held, held, sems + (None,), p, y, x, core, place, source)
 
     def block(self, slot, kind, core):
         return self.lower.at[slot, :, HALF * kind:HALF * (kind + 1)]
@@ -198,18 +207,14 @@
     def weights(self, act):
         act(1)
 
-    def spread(self, act, slot, kind):
+    def spread(self, act, slot, kind, first):
         for way in (1, 3, 2):
             act(self.along_x(slot, kind, way))
 
-    def weight_across(self, act, wait):
-        if wait:
-            for s in range(4):
-                for way in (1, 3, 2):
-                    self.arrived(s * 4 + (self.x + way) % 4, 1)
-
-    def run(self):
-        self.walk(lambda copy: copy.start(), True)
+    def weight_across(self):
+        for s in range(4):
+            for way in (1, 3, 2):
+                self.arrived(s * 4 + (self.x + way) % 4, 1)
 
 
 def chain(
@@ -218,9 +223,9 @@
     through_ref, through_in, through_out, first_sigma,
     rows_there, rows_here, gram_buf, end_buf, next_buf, next_out,
     part_out, part_in, part2_out, part2_in, pack, recv, rows_out,
-    load_sem, here_sem, ring_send, ring_recv, across_send, across_recv,
-    through_send, through_recv, through_sem, through_hop, ahead_sem,
-    end_sem, next_sem, part_sem, part2_sem, rows_sem, pack_send, pack_recv,
+    load_sem, here_sem, ring_send, ring_recv, across_sem,
+    through_recv, through_sem, through_hop, ahead_sem,
+    end_sem, next_sem, part_sem, part2_sem, rows_sem, pack_sem,
 ):
     parts = 8
     p = lax.axis_index("tm")
@@ -299,7 +304,7 @@
     end_copy.start()
     end_buf[my_rows] = end_ref[:, mine]
     ring = Ring(
-        lower_ref, weight_ref, (ring_send, ring_recv, across_send, across_recv),
+        lower_ref, weight_ref, (ring_send, ring_recv, across_sem),
         p, y, x, core, place, source_core)
 
     @pl.when(source_core)
@@ -315,21 +320,29 @@
             else:
                 weight_ref[chip] = both
 
-    ring.run()
-
-    @pl.loop(0, B // WINDOW)
-    def _(k):
-        columns = pl.ds(pl.multiple_of(k * WINDOW, WINDOW), WINDOW)
-        right = weight_ref[HALF_CHIPS:, :, columns].reshape(HALF, WINDOW)
-        total = dot(lower_ref[:, :, HALF:].reshape(HALF, HALF), right)
-        coupled_ref[:, :, columns] = total.astype(BF16).reshape(HALF_CHIPS, PANEL, WINDOW)
-
-        @pl.when(k < HALF // WINDOW)
-        def _():
-            left = weight_ref[:HALF_CHIPS, :, columns].reshape(HALF, WINDOW)
-            more = dot(lower_ref[:, :, :HALF].reshape(HALF, HALF), left) + total
-            coupled_ref[:, :, columns] = more.astype(BF16).reshape(HALF_CHIPS, PANEL, WINDOW)
-
+    def couple(s):
+        rows = pl.ds(4 * s, 4)
+        left = lower_ref[rows, :, :HALF].reshape(4 * PANEL, HALF)
+        right = lower_ref[rows, :, HALF:].reshape(4 * PANEL, HALF)
+        for k in range(B // WINDOW):
+            columns = slice(WINDOW * k, WINDOW * (k + 1))
+            total = dot(right, weight_ref[HALF_CHIPS:, :, columns].reshape(HALF, WINDOW))
+            if k < HALF // WINDOW:
+                total = total + dot(
+                    left, weight_ref[:HALF_CHIPS, :, columns].reshape(HALF, WINDOW))
+            coupled_ref[rows, :, columns] = total.astype(BF16).reshape(4, PANEL, WINDOW)
+
+    def couple_near():
+        ring.both_ways(lambda ours, others: others.wait_recv())
+
+        @pl.loop(1, 4)
+        def _(i):
+            couple((y + i) % 4)
+
+    ring.run(couple_near)
+    couple(y % 4)
+    ring.both_ways(lambda ours, others: ours.wait_send())
+    ring.finish()
     end_copy.wait_recv()
     end_b = end_buf[...].astype(BF16)
     broken = flag_ref[p] == 1
@@ -363,13 +376,22 @@
 
     def pack_copy(k, j):
         return pltpu.make_async_remote_copy(
-            src_ref=pack.at[k, j], dst_ref=recv.at[k, place], send_sem=pack_send.at[k, j],
-            recv_sem=pack_recv.at[k, place], device_id=peer(j), device_id_type=MESH)
-
-    def arrival(k, j):
-        return pltpu.make_async_remote_copy(
-            src_ref=pack.at[k, j], dst_ref=recv.at[k, j], send_sem=pack_send.at[k, j],
-            recv_sem=pack_recv.at[k, j], device_id=peer(j), device_id_type=MESH)
+            src_ref=pack.at[k, j], dst_ref=recv.at[k, place], send_sem=pack_sem.at[k, 0],
+            recv_sem=pack_sem.at[k, 1], device_id=peer(j), device_id_type=MESH)
+
+    def messages(k, act):
+        def count(n):
+            return pltpu.make_async_remote_copy(
+                src_ref=pack.at[k, :n], dst_ref=recv.at[k, :n], send_sem=pack_sem.at[k, 0],
+                recv_sem=pack_sem.at[k, 1], device_id=sibling, device_id_type=MESH)
+
+        @pl.when(source_core)
+        def _():
+            act(count(HALF_CHIPS - 1))
+
+        @pl.when(jnp.logical_not(source_core))
+        def _():
+            act(count(HALF_CHIPS))
 
     def emit(which, value, out_ref, act):
         copy = to_sibling(
@@ -395,11 +417,7 @@
                 recv[k, j] = pack[k, j]
 
         base = meanwhile(product)
-        for j in range(HALF_CHIPS):
-            @pl.when(jnp.logical_not(is_self(j)))
-            def _():
-                arrival(k, j).wait_recv()
-
+        messages(k, lambda copy: copy.wait_recv())
         first = recv[k, :, :16].reshape(HALF_CHIPS * 16, 128).T
         second = recv[k, :, 16:].reshape(HALF_CHIPS * 16, 128).T
 
@@ -418,7 +436,7 @@
         return sigma + part2_in[k]
 
     through_ring = PlainRing(
-        through_ref, (through_send, through_recv), p, y, x, core, place, source_core)
+        through_ref, (ring_send, through_recv), p, y, x, core, place, source_core)
     through_half = to_sibling(through_out, through_out, through_sem.at[0])
     through_here = to_sibling(through_out, through_ref.at[place, :, mine], through_sem.at[1])
     zero = jnp.zeros((PANEL, HALF), BF16)
@@ -467,7 +485,7 @@
         def _():
             to_sibling(through_out, through_ref.at[place, :, theirs], through_sem.at[1]).wait_recv()
 
-        through_ring.run()
+        through_ring.run(lambda: None)
 
     @pl.when(p < SPLIT - 2)
     def _():
@@ -553,18 +571,13 @@
     def _():
         here_copy.wait_send()
 
-    ring.finish()
-
     def sent(k):
         to_sibling(part_out.at[k], part_in.at[k], part_sem.at[k]).wait_send()
 
     def step_sent(k):
         sent(k)
         to_sibling(part2_out.at[k], part2_in.at[k], part2_sem.at[k]).wait_send()
-        for j in range(HALF_CHIPS):
-            @pl.when(jnp.logical_not(is_self(j)))
-            def _():
-                pack_copy(k, j).wait_send()
+        messages(k, lambda copy: copy.wait_send())
 
     step_sent(0)
 
@@ -632,13 +645,9 @@
             pltpu.VMEM((2, HALF_CHIPS, 32, 128), BF16),
             pltpu.VMEM((2, HALF_CHIPS, 32, 128), BF16),
             pltpu.VMEM((2, PANEL, HALF), F32),
-            dma((3,)), dma((2,)),
-            dma((HALF_CHIPS, 3, 5)), dma((HALF_CHIPS, 3)),
-            dma((HALF_CHIPS, 2)), dma((HALF_CHIPS, 2)),
-            dma((HALF_CHIPS, 2, 5)), dma((HALF_CHIPS, 2)),
-            dma((2, 2)), dma((2,)), dma((SPLIT,)),
-            dma((2,)), dma((3, 2)), dma((4, 2)), dma((2, 2)), dma((2, 2)),
-            dma((2, HALF_CHIPS)), dma((2, HALF_CHIPS)),
+            dma((3,)), dma((2,)), dma((75,)), dma((HALF_CHIPS, 3)), dma((2,)),
+            dma((HALF_CHIPS, 2)), dma((2, 2)), dma((2,)), dma((SPLIT,)),
+            dma((2,)), dma((3, 2)), dma((4, 2)), dma((2, 2)), dma((2, 2)), dma((2, 2)),
         ],
         compiler_params=pltpu.CompilerParams(
             collective_id=0, has_side_effects=True, vmem_limit_bytes=40 * 1024 * 1024),

time: 141 us -> 135 us (0.957)
  Pallas kernels: 135 us -> 129 us
    pallas_call x1, Pallas kernels: 135 us -> 129 us  [run_chain(): pl.pallas_call(chain, out_shape=[jax.ShapeDtypeStruct((OWN, B), F32)] * 2...]
where the time goes in v5:
time: 135 us; the launch traced here: 134 us
  Pallas kernels  129 us (96%)
  local copies, waits for them, and re-layouts  4.65 us (3%)
    pallas_call x1, Pallas kernels, run_chain(): pl.pallas_call(chain, out_shape=[jax.ShapeDtypeStruct((OWN, B), F32)] * 2...  129 us
    unnamed x10, local copies, waits for them, and re-layouts  4.65 us

profile of v5, /device:TPU:1, one launch (start us, length us, event | category | flops | bytes accessed | tf_op | source)
XLA Modules:
  0.0 134.4 jit_solution(10197298591790901216)
XLA Ops:
  0.6 0.0 copy-start.3
  0.6 0.6 copy-done.3
  1.3 0.0 copy-start
  1.3 0.9 copy-done
  2.2 0.0 copy-start.1
  2.2 0.9 copy-done.1
  3.1 0.0 copy-start.2
  3.1 0.9 copy-done.2
  4.0 129.1 %shard_map.59 = (f32[24,1536]{1,0:T(8,128)S(1)}, f32[24,1536]{1,0:T(8,128)S(1)}) custom-call(s32[8]{0:T(128)S(1)} %copy-done.3, bf16[24,1536]{1,0:T(8,128)(2,1)S(1)} %bitcast.6, bf16[24,1536]{1,0:T(8,128)(2,1)S(1)} %bitcast.7, f32[24,1536]{1,0:T(8,128)S(1)} %copy-done), custom_call_target="tpu_custom_call" | custom-call | tf_op jit(solution)/shard_map/pallas_call | solution.py:619
  133.1 0.7 copy.8
  133.7 0.7 copy.9
Async XLA Ops:
  0.6 0.7 copy-start.3
  1.3 0.9 copy-start
  2.2 0.9 copy-start.1
  3.1 0.9 copy-start.2

commit v6 on v5

--- a/solution.py
+++ b/solution.py
@@ -176,13 +176,13 @@
             self.row_sends(act, wait)
 
         self.weight_hop(act, wait, 1)
+        self.weight_hop(act, wait, 2)
         self.lower_hop(act, wait, 1, 0)
-        self.weight_hop(act, wait, 2)
         self.lower_hop(act, wait, 1, 1)
         self.weight_hop(act, wait, 3)
         self.lower_hop(act, wait, 2, 0)
+        self.lower_hop(act, wait, 2, 1)
         self.weight_hop(act, wait, 4)
-        self.lower_hop(act, wait, 2, 1)
         self.lower_hop(act, wait, 3, 0)
         self.lower_hop(act, wait, 3, 1)
 
@@ -220,7 +220,7 @@
 def chain(
     flag_ref, weight_hbm, lower_hbm, end_hbm, sigma_ref, cross_ref,
     weight_rows, lower_rows, end_ref, weight_ref, lower_ref, coupled_ref,
-    through_ref, through_in, through_out, first_sigma,
+    through_ref, through_in, through_out, first_sigma, cross_part, cross_in,
     rows_there, rows_here, gram_buf, end_buf, next_buf, next_out,
     part_out, part_in, part2_out, part2_in, pack, recv, rows_out,
     load_sem, here_sem, ring_send, ring_recv, across_sem,
@@ -408,13 +408,14 @@
         for j in range(HALF_CHIPS):
             pack[k, j] = message(product, j)
 
+        for j in range(HALF_CHIPS):
             @pl.when(jnp.logical_not(is_self(j)))
             def _():
                 pack_copy(k, j).start()
 
-            @pl.when(is_self(j))
-            def _():
-                recv[k, j] = pack[k, j]
+        @pl.when(source_core)
+        def _():
+            recv[k, place] = pack[k, place]
 
         base = meanwhile(product)
         messages(k, lambda copy: copy.wait_recv())
@@ -529,8 +530,8 @@
 
     @pl.when(p == SPLIT)
     def _():
-        for jump in jumps:
-            jump.start()
+        for q in (1, 2, 3, 0):
+            jumps[q].start()
 
     @pl.when(jnp.logical_not(early))
     def _():
@@ -563,7 +564,14 @@
             next_buf[2] = next_buf[1]
 
         source = jnp.where(broken, end_b, next_buf[2])
-        emit(0, -sum_halves(3, source, coupled_ref), cross_ref, "start")
+        for k in range(2):
+            columns = slice(HALF * k, HALF * (k + 1))
+            cross_part[:, columns] = -dot(
+                source, coupled_ref[:, :, columns].reshape(HALF, HALF))
+        cross_copy = to_sibling(cross_part.at[their_rows], cross_in, rows_sem.at[0])
+        cross_copy.start()
+        cross_copy.wait_recv()
+        cross_ref[...] = cross_part[my_rows] + cross_in[...]
 
     end_copy.wait_send()
 
@@ -593,7 +601,7 @@
     @pl.when(early)
     def _():
         step_sent(1)
-        sent(3)
+        to_sibling(cross_part.at[their_rows], cross_in, rows_sem.at[0]).wait_send()
 
         @pl.when(p > 0)
         def _():
@@ -609,7 +617,10 @@
         def _():
             through_here.wait_send()
 
-    emit(0, None, cross_ref, "wait")
+    @pl.when(jnp.logical_not(early))
+    def _():
+        emit(0, None, cross_ref, "wait")
+
     emit(1, None, sigma_ref, "wait")
 
 
@@ -632,14 +643,16 @@
             pltpu.VMEM((PANEL, HALF), BF16),
             pltpu.VMEM((PANEL, HALF), BF16),
             pltpu.VMEM((PANEL, HALF), F32),
+            pltpu.VMEM((PANEL, B), F32),
+            pltpu.VMEM((OWN, B), F32),
             pltpu.VMEM((2, OWN, B), F32),
             pltpu.VMEM((2, OWN, B), F32),
             pltpu.VMEM((WINDOW, B), F32),
             pltpu.VMEM((PANEL, HALF), F32),
             pltpu.VMEM((3, PANEL, HALF), BF16),
             pltpu.VMEM((2, PANEL, HALF), BF16),
-            pltpu.VMEM((4, PANEL, HALF), F32),
-            pltpu.VMEM((4, PANEL, HALF), F32),
+            pltpu.VMEM((3, PANEL, HALF), F32),
+            pltpu.VMEM((3, PANEL, HALF), F32),
             pltpu.VMEM((2, PANEL, HALF), F32),
             pltpu.VMEM((2, PANEL, HALF), F32),
             pltpu.VMEM((2, HALF_CHIPS, 32, 128), BF16),
@@ -647,7 +660,7 @@
             pltpu.VMEM((2, PANEL, HALF), F32),
             dma((3,)), dma((2,)), dma((75,)), dma((HALF_CHIPS, 3)), dma((2,)),
             dma((HALF_CHIPS, 2)), dma((2, 2)), dma((2,)), dma((SPLIT,)),
-            dma((2,)), dma((3, 2)), dma((4, 2)), dma((2, 2)), dma((2, 2)), dma((2, 2)),
+            dma((2,)), dma((3, 2)), dma((3, 2)), dma((2, 2)), dma((2, 2)), dma((2, 2)),
         ],
         compiler_params=pltpu.CompilerParams(
             collective_id=0, has_side_effects=True, vmem_limit_bytes=40 * 1024 * 1024),

time: 135 us -> 133 us (0.985)
  Pallas kernels: 129 us -> 127 us
    pallas_call x1, Pallas kernels: 129 us -> 127 us  [run_chain(): pl.pallas_call(chain, out_shape=[jax.ShapeDtypeStruct((OWN, B), F32)] * 2...]
where the time goes in v6:
time: 133 us
  Pallas kernels  127 us (95%)
  local copies, waits for them, and re-layouts  4.65 us (3%)
    pallas_call x1, Pallas kernels, run_chain(): pl.pallas_call(chain, out_shape=[jax.ShapeDtypeStruct((OWN, B), F32)] * 2...  127 us
    unnamed x10, local copies, waits for them, and re-layouts  4.65 us

profile of v6, /device:TPU:1, one launch (start us, length us, event | category | flops | bytes accessed | tf_op | source)
XLA Modules:
  0.0 132.6 jit_solution(9414958094637789187)
XLA Ops:
  0.6 0.0 copy-start.3
  0.6 0.6 copy-done.3
  1.3 0.0 copy-start
  1.3 0.9 copy-done
  2.2 0.0 copy-start.1
  2.2 0.9 copy-done.1
  3.1 0.0 copy-start.2
  3.1 0.9 copy-done.2
  4.0 127.3 %shard_map.59 = (f32[24,1536]{1,0:T(8,128)S(1)}, f32[24,1536]{1,0:T(8,128)S(1)}) custom-call(s32[8]{0:T(128)S(1)} %copy-done.3, bf16[24,1536]{1,0:T(8,128)(2,1)S(1)} %bitcast.6, bf16[24,1536]{1,0:T(8,128)(2,1)S(1)} %bitcast.7, f32[24,1536]{1,0:T(8,128)S(1)} %copy-done), custom_call_target="tpu_custom_call" | custom-call | tf_op jit(solution)/shard_map/pallas_call | solution.py:630
  131.2 0.7 copy.8
  131.9 0.7 copy.9
Async XLA Ops:
  0.6 0.7 copy-start.3
  1.3 0.9 copy-start
  2.2 0.9 copy-start.1
  3.1 0.9 copy-start.2

commit v7 on v6

--- a/solution.py
+++ b/solution.py
@@ -16,6 +16,8 @@
 HALF = 768
 WINDOW = 256
 SPLIT = 4
+STEP = 384
+LEFT = 1152
 
 
 def dot(a, b):
@@ -37,6 +39,8 @@
 
 
 class Ring:
+    later = (1, 2)
+
     def __init__(self, lower, weight, sems, p, y, x, core, place, source):
         self.lower, self.weight = lower, weight
         self.sends, self.receives, self.over = sems
@@ -44,13 +48,13 @@
         self.place, self.source = place, source
         self.sign = 1 - 2 * core
 
-    def block(self, slot, kind, core):
-        if kind == 0:
-            return self.lower.at[slot]
-        return self.weight.at[HALF_CHIPS * core + slot, :, HALF * (kind - 1):HALF * kind]
-
-    def copy(self, slot, kind, way, y, x):
-        block = self.block(slot, kind, self.core)
+    def block(self, slot, kind, pair):
+        if kind == 1:
+            return self.weight.at[HALF_CHIPS * self.core + slot, :, :STEP * (pair + 1)]
+        return self.lower.at[slot, :, slice(0, LEFT) if kind == 0 else slice(LEFT, B)]
+
+    def copy(self, slot, kind, pair, way, y, x):
+        block = self.block(slot, kind, pair)
         return pltpu.make_async_remote_copy(
             src_ref=block, dst_ref=block, send_sem=self.sends.at[self.sender(slot, kind, way)],
             recv_sem=self.receives.at[slot, kind],
@@ -61,12 +65,12 @@
             return 35 + 20 * (kind - 1) + 5 * (slot // 4) + way
         return 2 * slot + way if way < 2 else 30 + way
 
-    def along_x(self, slot, kind, way):
-        return self.copy(slot, kind, 1 + way, self.y, (self.x + way) % 4)
-
-    def along_y(self, slot, kind, back):
+    def along_x(self, slot, kind, pair, way):
+        return self.copy(slot, kind, pair, 1 + way, self.y, (self.x + way) % 4)
+
+    def along_y(self, slot, kind, pair, back):
         step = self.turn(slot, kind) * (-1 if back else 1)
-        return self.copy(slot, kind, back, (self.y + step + 8) % 8, self.x)
+        return self.copy(slot, kind, pair, back, (self.y + step + 8) % 8, self.x)
 
     def turn(self, slot, kind):
         return self.sign * (1 - 2 * (slot % 2)) if kind == 0 else self.sign
@@ -77,45 +81,52 @@
             src_ref=block, dst_ref=block, send_sem=self.over.at[0], recv_sem=self.over.at[1],
             device_id=(self.p, chip * 2 + 1 - self.core), device_id_type=MESH)
 
-    def arrived(self, slot, kind):
-        self.along_x(slot, kind, 1).wait_recv()
-
-    def weights(self, act):
-        act(1)
-
-        @pl.when(self.core == 1)
-        def _():
-            act(2)
-
-    def columns(self):
-        return [(self.x + i) % 4 for i in (0, 1, 3, 2)]
-
-    def spread(self, act, slot, kind, first):
+    def cross(self, slot, kind, pair):
+        if kind == 1:
+            self.across(self.block(slot, kind, pair)).start()
+
+    def arrived(self, slot, kind, pair):
+        self.along_x(slot, kind, pair, 1).wait_recv()
+
+    def of_row(self, origin, act):
+        for pair in range(4):
+            @pl.when(jnp.logical_and(origin // 2 == pair, self.core == pair // 2))
+            def _():
+                act(pair)
+
+    def spread(self, act, slot, kind, pair, first):
         for way in (1, 3, 2):
-            act(self.along_x(slot, kind, way))
-        if kind and first:
-            self.across(self.block(slot, kind, self.core)).start()
+            act(self.along_x(slot, kind, pair, way))
+        if first:
+            self.cross(slot, kind, pair)
+
+    def round_y(self, act, slot, kind, pair):
+        act(self.along_y(slot, kind, pair, 0))
+        act(self.along_y(slot, kind, pair, 1))
 
     def own_sends(self, act, first):
-        def round_y(kind):
-            act(self.along_y(self.place, kind, 0))
-            act(self.along_y(self.place, kind, 1))
-
-        self.spread(act, self.place, 0, first)
-        self.weights(round_y)
-        round_y(0)
-        self.weights(lambda kind: self.spread(act, self.place, kind, first))
+        def begin(pair):
+            for kind in self.later:
+                self.round_y(act, self.place, kind, pair)
+
+        def go_on(pair):
+            for kind in self.later:
+                self.spread(act, self.place, kind, pair, first)
+
+        self.spread(act, self.place, 0, None, False)
+        self.of_row(self.y, begin)
+        self.round_y(act, self.place, 0, None)
+        self.of_row(self.y, go_on)
 
     def row_sends(self, act, wait):
-        for column in self.columns()[1:]:
-            slot = (self.y % 4) * 4 + column
+        for around in (1, 3, 2):
+            slot = (self.y % 4) * 4 + (self.x + around) % 4
             if wait:
-                self.arrived(slot, 0)
-            act(self.along_y(slot, 0, 0))
-            act(self.along_y(slot, 0, 1))
-
-    def lower_hop(self, act, wait, distance, pair):
-        columns = [(self.x + pair) % 4, (self.x + pair + 2) % 4]
+                self.arrived(slot, 0, None)
+            self.round_y(act, slot, 0, None)
+
+    def lower_hop(self, act, wait, distance, odd):
+        columns = [(self.x + odd) % 4, (self.x + odd + 2) % 4]
         for back in range(2 if distance < 4 else 1):
             step = self.turn(columns[0], 0) * distance * (1 if back else -1)
             origin = (self.y + step + 8) % 8
@@ -125,41 +136,39 @@
                 for column in columns:
                     slot = (origin % 4) * 4 + column
                     if wait:
-                        self.arrived(slot, 0)
+                        self.arrived(slot, 0, None)
                     if distance < (3 if back else 4):
-                        act(self.along_y(slot, 0, back))
+                        act(self.along_y(slot, 0, None, back))
 
     def weight_hop(self, act, wait, distance):
         for back in range(2 if distance < 4 else 1):
             origin = (self.y + self.sign * distance * (1 if back else -1) + 8) % 8
-
-            @pl.when(origin // 4 == self.core)
-            def _():
-                slot = (origin % 4) * 4 + self.x
-
-                def pass_on(kind):
+            slot = (origin % 4) * 4 + self.x
+
+            def pass_on(pair):
+                for kind in self.later:
                     if wait:
-                        self.arrived(slot, kind)
+                        self.arrived(slot, kind, pair)
                     if distance < (3 if back else 4):
-                        act(self.along_y(slot, kind, back))
-                    self.spread(act, slot, kind, wait)
-
-                self.weights(pass_on)
-
-    def weight_across(self):
+                        act(self.along_y(slot, kind, pair, back))
+                    self.spread(act, slot, kind, pair, wait)
+
+            self.of_row(origin, pass_on)
+
+    def last_along_x(self):
         for s in range(4):
-            for way in (1, 3, 2):
-                slot = s * 4 + (self.x + way) % 4
-
-                def to_sibling(kind):
-                    self.arrived(slot, kind)
-                    self.across(self.block(slot, kind, self.core)).start()
-
-                self.weights(to_sibling)
+            def end(pair):
+                for way in (1, 3, 2):
+                    slot = s * 4 + (self.x + way) % 4
+                    for kind in self.later:
+                        self.arrived(slot, kind, pair)
+                        self.cross(slot, kind, pair)
+
+            self.of_row(4 * self.core + s, end)
 
     def both_ways(self, act):
-        lower_rows = self.weight.at[:HALF_CHIPS, :, :HALF]
-        upper_rows = self.weight.at[HALF_CHIPS:]
+        lower_rows = self.weight.at[:6]
+        upper_rows = self.weight.at[:14]
 
         @pl.when(self.core == 0)
         def _():
@@ -188,7 +197,7 @@
 
     def run(self, arrived):
         self.walk(lambda copy: copy.start(), True)
-        self.weight_across()
+        self.last_along_x()
         arrived()
         self.lower_hop(None, True, 4, 0)
         self.lower_hop(None, True, 4, 1)
@@ -198,23 +207,21 @@
 
 
 class PlainRing(Ring):
+    later = (1,)
+
     def __init__(self, held, sems, p, y, x, core, place, source):
         super().__init__(held, held, sems + (None,), p, y, x, core, place, source)
 
-    def block(self, slot, kind, core):
+    def block(self, slot, kind, pair):
         return self.lower.at[slot, :, HALF * kind:HALF * (kind + 1)]
 
-    def weights(self, act):
-        act(1)
-
-    def spread(self, act, slot, kind, first):
-        for way in (1, 3, 2):
-            act(self.along_x(slot, kind, way))
-
-    def weight_across(self):
-        for s in range(4):
-            for way in (1, 3, 2):
-                self.arrived(s * 4 + (self.x + way) % 4, 1)
+    def cross(self, slot, kind, pair):
+        pass
+
+    def of_row(self, origin, act):
+        @pl.when(origin // 4 == self.core)
+        def _():
+            act(None)
 
 
 def chain(
@@ -277,7 +284,9 @@
     expected = (
         6 + jnp.where(p > 0, 1, 0) + jnp.where(p < parts - 1, 1, 0)
         + jnp.where(p == SPLIT, SPLIT - 1, 0))
-    weight_ref[:HALF_CHIPS, :, HALF:] = jnp.zeros((HALF_CHIPS, PANEL, HALF), BF16)
+    for pair in range(3):
+        weight_ref[8 * pair:8 * pair + 8, :, STEP * (pair + 1):] = jnp.zeros(
+            (8, PANEL, B - STEP * (pair + 1)), BF16)
     for load in loads:
         load.wait()
     rows_here[0] = lower_rows[...].astype(F32)

time: 133 us -> 129 us (0.970)
  Pallas kernels: 127 us -> 124 us
    pallas_call x1, Pallas kernels: 127 us -> 124 us  [run_chain(): pl.pallas_call(chain, out_shape=[jax.ShapeDtypeStruct((OWN, B), F32)] * 2...]
where the time goes in v7:
time: 129 us
  Pallas kernels  124 us (96%)
  local copies, waits for them, and re-layouts  4.65 us (4%)
    pallas_call x1, Pallas kernels, run_chain(): pl.pallas_call(chain, out_shape=[jax.ShapeDtypeStruct((OWN, B), F32)] * 2...  124 us
    unnamed x10, local copies, waits for them, and re-layouts  4.65 us

profile of v7, /device:TPU:1, one launch (start us, length us, event | category | flops | bytes accessed | tf_op | source)
XLA Modules:
  0.0 129.2 jit_solution(4271500355331768777)
XLA Ops:
  0.6 0.0 copy-start.3
  0.6 0.6 copy-done.3
  1.3 0.0 copy-start
  1.3 0.9 copy-done
  2.2 0.0 copy-start.1
  2.2 0.9 copy-done.1
  3.1 0.0 copy-start.2
  3.1 0.9 copy-done.2
  4.0 123.9 %shard_map.59 = (f32[24,1536]{1,0:T(8,128)S(1)}, f32[24,1536]{1,0:T(8,128)S(1)}) custom-call(s32[8]{0:T(128)S(1)} %copy-done.3, bf16[24,1536]{1,0:T(8,128)(2,1)S(1)} %bitcast.6, bf16[24,1536]{1,0:T(8,128)(2,1)S(1)} %bitcast.7, f32[24,1536]{1,0:T(8,128)S(1)} %copy-done), custom_call_target="tpu_custom_call" | custom-call | tf_op jit(solution)/shard_map/pallas_call | solution.py:639
  127.9 0.7 copy.8
  128.5 0.7 copy.9
Async XLA Ops:
  0.6 0.7 copy-start.3
  1.3 0.9 copy-start
  2.2 0.9 copy-start.1
  3.1 0.9 copy-start.2

commit v8 on v7

--- a/solution.py
+++ b/solution.py
@@ -363,13 +363,21 @@
             device_id=(target, r), device_id_type=MESH)
 
     below = jnp.maximum(p - 1, 0)
-    hops = [
-        down(next_out.at[0], next_buf.at[0], next_sem.at[0, 0], next_sem.at[0, 1], below),
-        None,
-        down(next_out.at[1], next_buf.at[2], next_sem.at[2, 0], next_sem.at[2, 1], below),
-    ]
+    pieces = (slice(0, 512), slice(512, HALF))
+
+    def hop(which, held, c):
+        return down(
+            next_out.at[held, :, pieces[c]], next_buf.at[which, :, pieces[c]],
+            next_sem.at[which, 0, c], next_sem.at[which, 1, c], below)
+
+    hops = [[hop(0, 0, 0), hop(0, 0, 1)], None, [hop(2, 1, 0), hop(2, 1, 1)]]
     jumps = [
-        down(next_out.at[0], next_buf.at[1], ahead_sem.at[q], next_sem.at[1, 1], q)
+        [
+            down(
+                next_out.at[0, :, piece], next_buf.at[1, :, piece],
+                ahead_sem.at[q, c], next_sem.at[1, 1, c], q)
+            for c, piece in enumerate(pieces)
+        ]
         for q in range(SPLIT)
     ]
     through_copy = down(
@@ -412,7 +420,12 @@
         else:
             copy.wait()
 
-    def step(k, source, right_ref, meanwhile):
+    def part2_copy(k, c):
+        piece = pieces[c]
+        return to_sibling(
+            part2_out.at[k, :, piece], part2_in.at[k, :, piece], part2_sem.at[k, c])
+
+    def step(k, source, right_ref, meanwhile, finish):
         product = sum_halves(k, source, right_ref)
         for j in range(HALF_CHIPS):
             pack[k, j] = message(product, j)
@@ -431,19 +444,23 @@
         first = recv[k, :, :16].reshape(HALF_CHIPS * 16, 128).T
         second = recv[k, :, 16:].reshape(HALF_CHIPS * 16, 128).T
 
-        def update(columns):
+        def update(side, piece):
+            width = piece.stop - piece.start
+            columns = pl.ds(pl.multiple_of(side * HALF + piece.start, 128), width)
+
             def rows(i):
-                return right_ref[:, 16 * i:16 * i + 16, columns].reshape(HALF_CHIPS * 16, HALF)
+                return right_ref[:, 16 * i:16 * i + 16, columns].reshape(HALF_CHIPS * 16, width)
             total = dot(first[:48], rows(0)) + dot(first[64:112], rows(1))
             total = total + dot(second[:48], rows(2))
             return total if base is None else total + base(columns)
 
-        copy = to_sibling(part2_out.at[k], part2_in.at[k], part2_sem.at[k])
-        part2_out[k] = update(theirs)
-        copy.start()
-        sigma = update(mine)
-        copy.wait_recv()
-        return sigma + part2_in[k]
+        for c, piece in enumerate(pieces):
+            part2_out[k, :, piece] = update(1 - core, piece)
+            part2_copy(k, c).start()
+        for c, piece in enumerate(pieces):
+            sigma = update(core, piece)
+            part2_copy(k, c).wait_recv()
+            finish(c, piece, sigma + part2_in[k, :, piece])
 
     through_ring = PlainRing(
         through_ref, (ring_send, through_recv), p, y, x, core, place, source_core)
@@ -505,7 +522,8 @@
 
     @pl.when(has_above)
     def _():
-        hops[0].wait_recv()
+        hops[0][0].wait_recv()
+        hops[0][1].wait_recv()
 
     @pl.when(jnp.logical_not(has_above))
     def _():
@@ -529,44 +547,54 @@
 
         return lambda columns: gram_buf[gram_rows, columns]
 
-    sigma = step(0, jnp.where(use_end, end_b, next_buf[0]), coupled_ref, gram)
-    next_out[0] = sigma.astype(BF16)
     sends_down = jnp.logical_and(p > 0, p != SPLIT)
 
-    @pl.when(sends_down)
-    def _():
-        hops[0].start()
-
-    @pl.when(p == SPLIT)
-    def _():
-        for q in (1, 2, 3, 0):
-            jumps[q].start()
+    def pass_first(c, piece, sigma):
+        next_out[0, :, piece] = sigma.astype(BF16)
+
+        @pl.when(sends_down)
+        def _():
+            hops[0][c].start()
+
+        @pl.when(p == SPLIT)
+        def _():
+            for q in (1, 2, 3, 0):
+                jumps[q][c].start()
+
+        first_sigma[:, piece] = sigma
+
+    step(0, jnp.where(use_end, end_b, next_buf[0]), coupled_ref, gram, pass_first)
 
     @pl.when(jnp.logical_not(early))
     def _():
-        emit(1, sigma, sigma_ref, "start")
+        emit(1, first_sigma[...], sigma_ref, "start")
 
     @pl.when(early)
     def _():
-        first_sigma[...] = sigma
-
         @pl.when(p == SPLIT - 2)
         def _():
             gather_through()
 
-        jumps[0].wait_recv()
-        whole = first_sigma[...] + step(1, next_buf[1], through_ref, lambda product: None)
-        next_out[1] = whole.astype(BF16)
-
-        @pl.when(p > 0)
-        def _():
-            hops[2].start()
-
-        emit(1, whole, sigma_ref, "start")
+        jumps[0][0].wait_recv()
+        jumps[0][1].wait_recv()
+
+        def pass_whole(c, piece, sigma):
+            whole = first_sigma[:, piece] + sigma
+            next_out[1, :, piece] = whole.astype(BF16)
+
+            @pl.when(p > 0)
+            def _():
+                hops[2][c].start()
+
+            first_sigma[:, piece] = whole
+
+        step(1, next_buf[1], through_ref, lambda product: None, pass_whole)
+        emit(1, first_sigma[...], sigma_ref, "start")
 
         @pl.when(p < SPLIT - 1)
         def _():
-            hops[2].wait_recv()
+            hops[2][0].wait_recv()
+            hops[2][1].wait_recv()
 
         @pl.when(p == SPLIT - 1)
         def _():
@@ -593,19 +621,22 @@
 
     def step_sent(k):
         sent(k)
-        to_sibling(part2_out.at[k], part2_in.at[k], part2_sem.at[k]).wait_send()
+        part2_copy(k, 0).wait_send()
+        part2_copy(k, 1).wait_send()
         messages(k, lambda copy: copy.wait_send())
 
     step_sent(0)
 
     @pl.when(sends_down)
     def _():
-        hops[0].wait_send()
+        hops[0][0].wait_send()
+        hops[0][1].wait_send()
 
     @pl.when(p == SPLIT)
     def _():
         for jump in jumps:
-            jump.wait_send()
+            jump[0].wait_send()
+            jump[1].wait_send()
 
     @pl.when(early)
     def _():
@@ -615,7 +646,8 @@
         @pl.when(p > 0)
         def _():
             through_copy.wait_send()
-            hops[2].wait_send()
+            hops[2][0].wait_send()
+            hops[2][1].wait_send()
 
     @pl.when(p < SPLIT - 1)
     def _():
@@ -668,8 +700,8 @@
             pltpu.VMEM((2, HALF_CHIPS, 32, 128), BF16),
             pltpu.VMEM((2, PANEL, HALF), F32),
             dma((3,)), dma((2,)), dma((75,)), dma((HALF_CHIPS, 3)), dma((2,)),
-            dma((HALF_CHIPS, 2)), dma((2, 2)), dma((2,)), dma((SPLIT,)),
-            dma((2,)), dma((3, 2)), dma((3, 2)), dma((2, 2)), dma((2, 2)), dma((2, 2)),
+            dma((HALF_CHIPS, 2)), dma((2, 2)), dma((2,)), dma((SPLIT, 2)),
+            dma((2,)), dma((3, 2, 2)), dma((3, 2)), dma((2, 2, 2)), dma((2, 2)), dma((2, 2)),
         ],
         compiler_params=pltpu.CompilerParams(
             collective_id=0, has_side_effects=True, vmem_limit_bytes=40 * 1024 * 1024),

time: 129 us -> 131 us (1.016)
  Pallas kernels: 124 us -> 126 us
    pallas_call x1, Pallas kernels: 124 us -> 126 us  [run_chain(): pl.pallas_call(chain, out_shape=[jax.ShapeDtypeStruct((OWN, B), F32)] * 2...]
where the time goes in v8:
time: 131 us
  Pallas kernels  126 us (96%)
  local copies, waits for them, and re-layouts  4.65 us (4%)
    pallas_call x1, Pallas kernels, run_chain(): pl.pallas_call(chain, out_shape=[jax.ShapeDtypeStruct((OWN, B), F32)] * 2...  126 us
    unnamed x10, local copies, waits for them, and re-layouts  4.65 us

profile of v8, /device:TPU:1, one launch (start us, length us, event | category | flops | bytes accessed | tf_op | source)
XLA Modules:
  0.0 131.1 jit_solution(4166443391089148257)
XLA Ops:
  0.6 0.0 copy-start.3
  0.6 0.6 copy-done.3
  1.3 0.0 copy-start
  1.3 0.9 copy-done
  2.2 0.0 copy-start.1
  2.2 0.9 copy-done.1
  3.1 0.0 copy-start.2
  3.1 0.9 copy-done.2
  4.0 125.8 %shard_map.59 = (f32[24,1536]{1,0:T(8,128)S(1)}, f32[24,1536]{1,0:T(8,128)S(1)}) custom-call(s32[8]{0:T(128)S(1)} %copy-done.3, bf16[24,1536]{1,0:T(8,128)(2,1)S(1)} %bitcast.6, bf16[24,1536]{1,0:T(8,128)(2,1)S(1)} %bitcast.7, f32[24,1536]{1,0:T(8,128)S(1)} %copy-done), custom_call_target="tpu_custom_call" | custom-call | tf_op jit(solution)/shard_map/pallas_call | solution.py:671
  129.7 0.7 copy.8
  130.4 0.7 copy.9
Async XLA Ops:
  0.6 0.7 copy-start.3
  1.3 0.9 copy-start
  2.2 0.9 copy-start.1
  3.1 0.9 copy-start.2

commit v9 on v7

--- a/solution.py
+++ b/solution.py
@@ -350,8 +350,11 @@
 
     ring.run(couple_near)
     couple(y % 4)
-    ring.both_ways(lambda ours, others: ours.wait_send())
-    ring.finish()
+
+    def ring_sent():
+        ring.both_ways(lambda ours, others: ours.wait_send())
+        ring.finish()
+
     end_copy.wait_recv()
     end_b = end_buf[...].astype(BF16)
     broken = flag_ref[p] == 1
@@ -491,6 +494,8 @@
             through_here.start()
 
     def gather_through():
+        ring_sent()
+
         @pl.when(source_core)
         def _():
             to_sibling(through_out, through_ref.at[place, :, theirs], through_sem.at[1]).wait_recv()
@@ -512,6 +517,15 @@
         next_buf[0] = zero
 
     use_end = jnp.logical_or(broken, p == parts - 1)
+
+    def settle(product):
+        @pl.when(p < SPLIT - 1)
+        def _():
+            through_ring.finish()
+
+        @pl.when(p == SPLIT - 1)
+        def _():
+            ring_sent()
 
     def gram(product):
         window = jnp.minimum(chip * PANEL // 128, (B - WINDOW) // 128) * 128
@@ -555,7 +569,7 @@
             gather_through()
 
         jumps[0].wait_recv()
-        whole = first_sigma[...] + step(1, next_buf[1], through_ref, lambda product: None)
+        whole = first_sigma[...] + step(1, next_buf[1], through_ref, settle)
         next_out[1] = whole.astype(BF16)
 
         @pl.when(p > 0)
@@ -620,7 +634,6 @@
     @pl.when(p < SPLIT - 1)
     def _():
         sent(2)
-        through_ring.finish()
 
         @pl.when(jnp.logical_not(source_core))
         def _():
@@ -628,6 +641,7 @@
 
     @pl.when(jnp.logical_not(early))
     def _():
+        ring_sent()
         emit(0, None, cross_ref, "wait")
 
     emit(1, None, sigma_ref, "wait")

time: 129 us -> 129 us (level)
  no operation moved by 1% of the time
where the time goes in v9:
time: 129 us
  Pallas kernels  123 us (95%)
  local copies, waits for them, and re-layouts  4.65 us (4%)
    pallas_call x1, Pallas kernels, run_chain(): pl.pallas_call(chain, out_shape=[jax.ShapeDtypeStruct((OWN, B), F32)] * 2...  123 us
    unnamed x10, local copies, waits for them, and re-layouts  4.65 us

profile of v9, /device:TPU:1, one launch (start us, length us, event | category | flops | bytes accessed | tf_op | source)
XLA Modules:
  0.0 128.7 jit_solution(14279670052812188082)
XLA Ops:
  0.6 0.0 copy-start.3
  0.6 0.6 copy-done.3
  1.3 0.0 copy-start
  1.3 0.9 copy-done
  2.2 0.0 copy-start.1
  2.2 0.9 copy-done.1
  3.1 0.0 copy-start.2
  3.1 0.9 copy-done.2
  4.0 123.4 %shard_map.59 = (f32[24,1536]{1,0:T(8,128)S(1)}, f32[24,1536]{1,0:T(8,128)S(1)}) custom-call(s32[8]{0:T(128)S(1)} %copy-done.3, bf16[24,1536]{1,0:T(8,128)(2,1)S(1)} %bitcast.6, bf16[24,1536]{1,0:T(8,128)(2,1)S(1)} %bitcast.7, f32[24,1536]{1,0:T(8,128)S(1)} %copy-done), custom_call_target="tpu_custom_call" | custom-call | tf_op jit(solution)/shard_map/pallas_call | solution.py:653
  127.4 0.7 copy.8
  128.1 0.7 copy.9
Async XLA Ops:
  0.6 0.7 copy-start.3
  1.3 0.9 copy-start
  2.2 0.9 copy-start.1
  3.1 0.9 copy-start.2

commit v10 on v9

--- a/solution.py
+++ b/solution.py
@@ -333,13 +333,13 @@
         rows = pl.ds(4 * s, 4)
         left = lower_ref[rows, :, :HALF].reshape(4 * PANEL, HALF)
         right = lower_ref[rows, :, HALF:].reshape(4 * PANEL, HALF)
-        for k in range(B // WINDOW):
-            columns = slice(WINDOW * k, WINDOW * (k + 1))
-            total = dot(right, weight_ref[HALF_CHIPS:, :, columns].reshape(HALF, WINDOW))
-            if k < HALF // WINDOW:
+        for k in range(B // HALF):
+            columns = slice(HALF * k, HALF * (k + 1))
+            total = dot(right, weight_ref[HALF_CHIPS:, :, columns].reshape(HALF, HALF))
+            if k < HALF // HALF:
                 total = total + dot(
-                    left, weight_ref[:HALF_CHIPS, :, columns].reshape(HALF, WINDOW))
-            coupled_ref[rows, :, columns] = total.astype(BF16).reshape(4, PANEL, WINDOW)
+                    left, weight_ref[:HALF_CHIPS, :, columns].reshape(HALF, HALF))
+            coupled_ref[rows, :, columns] = total.astype(BF16).reshape(4, PANEL, HALF)
 
     def couple_near():
         ring.both_ways(lambda ours, others: others.wait_recv())
@@ -518,6 +518,11 @@
 
     use_end = jnp.logical_or(broken, p == parts - 1)
 
+    def cross_copy(k):
+        columns = slice(HALF * k, HALF * (k + 1))
+        return to_sibling(
+            cross_part.at[their_rows, columns], cross_in.at[:, columns], rows_sem.at[2 * k])
+
     def settle(product):
         @pl.when(p < SPLIT - 1)
         def _():
@@ -591,9 +596,9 @@
             columns = slice(HALF * k, HALF * (k + 1))
             cross_part[:, columns] = -dot(
                 source, coupled_ref[:, :, columns].reshape(HALF, HALF))
-        cross_copy = to_sibling(cross_part.at[their_rows], cross_in, rows_sem.at[0])
-        cross_copy.start()
-        cross_copy.wait_recv()
+            cross_copy(k).start()
+        for k in range(2):
+            cross_copy(k).wait_recv()
         cross_ref[...] = cross_part[my_rows] + cross_in[...]
 
     end_copy.wait_send()
@@ -624,7 +629,8 @@
     @pl.when(early)
     def _():
         step_sent(1)
-        to_sibling(cross_part.at[their_rows], cross_in, rows_sem.at[0]).wait_send()
+        cross_copy(0).wait_send()
+        cross_copy(1).wait_send()
 
         @pl.when(p > 0)
         def _():
@@ -683,7 +689,7 @@
             pltpu.VMEM((2, PANEL, HALF), F32),
             dma((3,)), dma((2,)), dma((75,)), dma((HALF_CHIPS, 3)), dma((2,)),
             dma((HALF_CHIPS, 2)), dma((2, 2)), dma((2,)), dma((SPLIT,)),
-            dma((2,)), dma((3, 2)), dma((3, 2)), dma((2, 2)), dma((2, 2)), dma((2, 2)),
+            dma((2,)), dma((3, 2)), dma((3, 2)), dma((2, 2)), dma((3, 2)), dma((2, 2)),
         ],
         compiler_params=pltpu.CompilerParams(
             collective_id=0, has_side_effects=True, vmem_limit_bytes=40 * 1024 * 1024),

time: 129 us -> 129 us (level)
  no operation moved by 1% of the time
where the time goes in v10:
time: 129 us
  Pallas kernels  124 us (96%)
  local copies, waits for them, and re-layouts  4.65 us (4%)
    pallas_call x1, Pallas kernels, run_chain(): pl.pallas_call(chain, out_shape=[jax.ShapeDtypeStruct((OWN, B), F32)] * 2...  124 us
    unnamed x10, local copies, waits for them, and re-layouts  4.65 us

profile of v10, /device:TPU:1, one launch (start us, length us, event | category | flops | bytes accessed | tf_op | source)
XLA Modules:
  0.0 128.9 jit_solution(13871539507640786908)
XLA Ops:
  0.6 0.0 copy-start.3
  0.6 0.6 copy-done.3
  1.3 0.0 copy-start
  1.3 0.9 copy-done
  2.2 0.0 copy-start.1
  2.2 0.9 copy-done.1
  3.1 0.0 copy-start.2
  3.1 0.9 copy-done.2
  4.0 123.6 %shard_map.59 = (f32[24,1536]{1,0:T(8,128)S(1)}, f32[24,1536]{1,0:T(8,128)S(1)}) custom-call(s32[8]{0:T(128)S(1)} %copy-done.3, bf16[24,1536]{1,0:T(8,128)(2,1)S(1)} %bitcast.6, bf16[24,1536]{1,0:T(8,128)(2,1)S(1)} %bitcast.7, f32[24,1536]{1,0:T(8,128)S(1)} %copy-done), custom_call_target="tpu_custom_call" | custom-call | tf_op jit(solution)/shard_map/pallas_call | solution.py:659
  127.6 0.7 copy.8
  128.2 0.7 copy.9
Async XLA Ops:
  0.6 0.7 copy-start.3
  1.3 0.9 copy-start
  2.2 0.9 copy-start.1
  3.1 0.9 copy-start.2

commit v11 on v9

--- a/solution.py
+++ b/solution.py
@@ -553,7 +553,7 @@
 
     @pl.when(p == SPLIT)
     def _():
-        for q in (1, 2, 3, 0):
+        for q in (1, 0, 2, 3):
             jumps[q].start()
 
     @pl.when(jnp.logical_not(early))

time: 129 us -> 129 us (level)
  no operation moved by 1% of the time
where the time goes in v11:
time: 129 us
  Pallas kernels  123 us (95%)
  local copies, waits for them, and re-layouts  4.65 us (4%)
    pallas_call x1, Pallas kernels, run_chain(): pl.pallas_call(chain, out_shape=[jax.ShapeDtypeStruct((OWN, B), F32)] * 2...  123 us
    unnamed x10, local copies, waits for them, and re-layouts  4.65 us

profile of v11, /device:TPU:1, one launch (start us, length us, event | category | flops | bytes accessed | tf_op | source)
XLA Modules:
  0.0 128.7 jit_solution(516238072352438185)
XLA Ops:
  0.6 0.0 copy-start.3
  0.6 0.6 copy-done.3
  1.3 0.0 copy-start
  1.3 0.9 copy-done
  2.2 0.0 copy-start.1
  2.2 0.9 copy-done.1
  3.1 0.0 copy-start.2
  3.1 0.9 copy-done.2
  4.0 123.4 %shard_map.59 = (f32[24,1536]{1,0:T(8,128)S(1)}, f32[24,1536]{1,0:T(8,128)S(1)}) custom-call(s32[8]{0:T(128)S(1)} %copy-done.3, bf16[24,1536]{1,0:T(8,128)(2,1)S(1)} %bitcast.6, bf16[24,1536]{1,0:T(8,128)(2,1)S(1)} %bitcast.7, f32[24,1536]{1,0:T(8,128)S(1)} %copy-done), custom_call_target="tpu_custom_call" | custom-call | tf_op jit(solution)/shard_map/pallas_call | solution.py:653
  127.4 0.7 copy.8
  128.1 0.7 copy.9
Async XLA Ops:
  0.6 0.7 copy-start.3
  1.3 0.9 copy-start
  2.2 0.9 copy-start.1
  3.1 0.9 copy-start.2
